TPU v7x, 512 devices: a whole 4x8x8 slice. The times are simulated.
512 devices in a mesh: elem: 32 (over x, z_hi, core), range: 16 (over y, z_lo).
Axes of the slice: x: 4, y: 8, z: 8 (z_hi: 4, z_lo: 2; z = z_hi * 2 + z_lo), core: 2. Of those that a mesh axis runs over, the one named last changes fastest.
Arguments:
- echoes: bfloat16 [2, 4096, 32, 4096], P(None, 'elem', 'range'), may hold values from -6 to 6
- steer_table: bfloat16 [2, 128, 4096], P(None, None, 'elem'), may hold values from -0.0625 to 0.0625
- beam_index: int32 [64], replicated, may hold values from 0 to 127
- pulse_code: bfloat16 [2, 256], replicated, may hold values from -0.25 to 0.25
- clutter_taps: float32 [2, 2], replicated, may hold values from 0.3 to 0.9
- dilation: int32 [2], replicated, may hold values from 1 to 3, as said below
Outputs:
- filtered: float32 [64, 2, 32, 4096], P('elem', None, None, 'range')
Inputs may be any that keep to these rules, and one draw needn't show every extreme that they name: `dilation`: the 2 sections have distinct spacings, the largest of them 3.
All inputs are finite; a program needn't handle non-finite values.
Results may differ from a plain program's by a relative error of at most 0.019.
Values may be sent and summed in bfloat16 or wider, within the bound.
No kernel may reach another device: no remote copies, remote signals or barrier semaphores. Data moves between devices by JAX's collectives and lax.ppermute only.
A program may use at most 64 MiB of HBM per device.

v0:
```python
import jax
import jax.numpy as jnp
from jax import lax
from jax.sharding import PartitionSpec as P


def passed_along(block, axis, distance):
    devices = range(lax.axis_size(axis))
    route = [(i - distance, i) for i in devices if i - distance in devices]
    return lax.ppermute(block, axis, route)


def toeplitz_band(coefficients, slab_width, length):
    tap_count = coefficients.shape[0]
    padded_code = jnp.concatenate(
        [coefficients, jnp.zeros((length + 1 - tap_count,), coefficients.dtype)]
    )
    return jnp.tile(padded_code, slab_width)[: slab_width * length].reshape(slab_width, length).T


def compress(signal, pulse_code, slab_width):
    local_beams = signal.shape[0]
    pulse_count = signal.shape[2]
    length = signal.shape[3]
    real_band = toeplitz_band(pulse_code[0], slab_width, length)
    imag_band = toeplitz_band(pulse_code[1], slab_width, length)
    matrix = jnp.concatenate(
        [jnp.concatenate([real_band, -imag_band], 1), jnp.concatenate([imag_band, real_band], 1)], 0
    )
    pulse_rows = signal.transpose(0, 2, 1, 3).reshape(local_beams * pulse_count, 2 * length)
    product = jnp.dot(pulse_rows, matrix, preferred_element_type=jnp.float32)
    return product.reshape(local_beams, pulse_count, 2, slab_width).transpose(0, 2, 1, 3)


def delayed(values, spacing):
    pulse_count = values.shape[2]
    rolled = jnp.roll(values, spacing, axis=2)
    inside = (jnp.arange(pulse_count, dtype=jnp.int32) >= spacing)[:, None]
    return jnp.where(inside, rolled, jnp.zeros_like(rolled))


def on_device(echoes, steer_table, beam_index, pulse_code, clutter_taps, dilation):
    range_count = lax.axis_size("range")
    beam_count = beam_index.shape[0]
    elem_dev = echoes.shape[1]
    pulse_dev = echoes.shape[2]
    gate_count = echoes.shape[3]
    slab_width = gate_count // range_count
    selector = (
        beam_index[:, None] == jnp.arange(steer_table.shape[1], dtype=jnp.int32)[None, :]
    ).astype(jnp.bfloat16)
    samples = echoes.reshape(2 * elem_dev, pulse_dev * gate_count)
    real_w = jnp.dot(selector, steer_table[0], preferred_element_type=jnp.float32).astype(
        jnp.bfloat16
    )
    imag_w = jnp.dot(selector, steer_table[1], preferred_element_type=jnp.float32).astype(
        jnp.bfloat16
    )
    stacked = jnp.stack(
        [jnp.concatenate([real_w, -imag_w], 1), jnp.concatenate([imag_w, real_w], 1)], 1
    )
    stacked = stacked.reshape(2 * beam_count, 2 * elem_dev)
    product = jnp.dot(stacked, samples, preferred_element_type=jnp.float32)
    partial_terms = product.reshape(beam_count, 2, pulse_dev, gate_count).astype(jnp.bfloat16)
    regrouped = lax.all_to_all(partial_terms, "range", split_axis=3, concat_axis=2, tiled=True)
    signal = lax.psum_scatter(
        regrouped.astype(jnp.float32).astype(jnp.bfloat16), "elem", scatter_dimension=0, tiled=True
    )
    following = passed_along(signal, "range", -1)
    signal = jnp.concatenate([signal, following], axis=3)
    filtered = compress(signal, pulse_code, slab_width)
    for section_index in range(clutter_taps.shape[0]):
        spacing = dilation[section_index]
        filtered = (
            filtered
            - clutter_taps[section_index, 0] * delayed(filtered, spacing)
            - clutter_taps[section_index, 1] * delayed(filtered, 2 * spacing)
        )
    return filtered


def solution(mesh):
    placed = (P(None, "elem", "range", None), P(None, None, "elem"), P(), P(), P(), P())
    return jax.shard_map(
        on_device,
        mesh=mesh,
        in_specs=placed,
        out_specs=P("elem", None, None, "range"),
        check_vma=False,
    )
```

profile of v0, /device:TPU:88, one launch (start us, length us, event | category | flops | bytes accessed | tf_op | source)
XLA Modules:
  0.0 238.6 jit_solution(9904258576959249440)
XLA Ops:
  6.5 0.0 reduce-scatter.2.cloned.1.call-start
  6.5 1.0 fusion.28
  7.5 1.0 convolution_convert_fusion.2
  8.5 8.6 %copy.25 = bf16[32,8,2,4096]{3,1,2,0:T(8,128)(2,1)} copy(bf16[32,8,2,4096]{3,2,1,0:T(2,128)(2,1)} %bitcast.61) | data formatting | bytes 8388608
  17.1 6.4 %copy.15 = bf16[8192,256]{1,0:T(8,128)(2,1)} copy(bf16[8192,256]{0,1:T(8,128)(2,1)} %bitcast.58) | data formatting | bytes 8388608 | tf_op jit(solution)/shard_map/dot_general | solution.py:63
  23.5 3.7 %convolution_convert_fusion = bf16[64,2,2,4096]{3,0,2,1:T(8,128)(2,1)S(1)} fusion(bf16[2,4096,256,1]{2,1,0,3:T(8,128)(2,1)} %bitcast.57, bf16[64,1,256]{2,0,1:T(8,128)(2,1)S(1)} %get-tuple-element.9, bf16[64,1,256]{2,0,1:T(8,128)(2,1)S(1)} %get-tuple-element.8), kind=kOutput, calls=%fused_computation | convolution fusion | flops 538050560 | bytes 6356992 | tf_op jit(solution)/shard_map/dot_general | solution.py:63
  27.2 7.3 %copy.16 = bf16[64,2,2,4096]{0,2,1,3:T(2,128)(2,1)} copy(bf16[64,2,2,4096]{3,0,2,1:T(8,128)(2,1)S(1)} %convolution_convert_fusion) | data formatting | bytes 4194304 | tf_op jit(solution)/shard_map/convert_element_type | solution.py:64
  34.5 6.3 %reshape.32 = bf16[16,2,32768]{2,1,0:T(2,128)(2,1)S(1)} reshape(bf16[4096,2,2,64]{3,2,1,0:T(2,128)(2,1)} %bitcast.55) | data formatting | bytes 4194304
  40.8 56.1 %all_to_all.18 = bf16[16,2,32768]{2,1,0:T(2,128)(2,1)} all-to-all(bf16[16,2,32768]{2,1,0:T(2,128)(2,1)S(1)} %reshape.32), channel_id=1, replica_groups=mesh['elem'=32,'range'=16] {'range'}, dimensions={0} | all-to-all | bytes 4194304 | tf_op jit(solution)/shard_map/all_to_all | solution.py:65
  96.9 7.4 %reshape.33 = bf16[4096,2,2,64]{3,2,1,0:T(2,128)(2,1)} reshape(bf16[16,2,32768]{2,1,0:T(2,128)(2,1)} %all_to_all.18) | data formatting | bytes 4194304
  104.3 8.9 %copy.24 = bf16[64,2,2,16,256]{4,0,2,3,1:T(8,128)(2,1)S(1)} copy(bf16[64,2,2,16,256]{0,2,1,4,3:T(2,128)(2,1)} %bitcast.56) | data formatting | bytes 4194304 | tf_op jit(solution)/shard_map/all_to_all | solution.py:65
  113.2 2.5 %copy.19 = bf16[64,2,32,256]{3,2,1,0:T(8,128)(2,1)} copy(bf16[64,2,32,256]{3,0,2,1:T(8,128)(2,1)S(1)} %bitcast.59) | data formatting | bytes 4194304 | tf_op jit(solution)/shard_map/all_to_all | solution.py:65
  115.8 0.0 copy-start.2
  115.8 0.0 copy-start
  115.8 0.0 reduce-scatter.2.cloned.1.call-update
  115.8 0.6 copy-done.2
  116.4 0.0 copy-start.1
  116.4 0.6 fusion.27
  121.8 0.0 copy-done
  121.9 0.6 tile.21
  122.5 0.2 reshape.24
  122.7 0.6 tile.9
  123.4 0.2 reshape.23
  123.6 0.7 iota_compare_fusion.5
  124.2 0.0 copy-done.1
  124.2 0.7 fusion.26
  124.9 0.1 maximum_maximum_fusion
  125.1 93.2 %reduce-scatter.2.cloned.1.call-done = bf16[2,2,32,256]{3,2,1,0:T(8,128)(2,1)} async-done(((bf16[64,2,32,256]{3,2,1,0:T(8,128)(2,1)}), bf16[2,2,32,256]{3,2,1,0:T(8,128)(2,1)}) %reduce-scatter.2.cloned.1.call-update) | async-done | bytes 65552 | tf_op jit(solution)/shard_map/reduce_scatter | solution.py:66
  218.3 3.1 %collective-permute-start = (bf16[2,2,32,256]{3,2,1,0:T(8,128)(2,1)}, bf16[2,2,32,256]{3,2,1,0:T(8,128)(2,1)S(1)}, u32[]{:S(2)}, u32[]{:S(2)}) collective-permute-start(bf16[2,2,32,256]{3,2,1,0:T(8,128)(2,1)} %reduce-scatter.2.cloned.1.call-done), channel_id=1, source_target_pairs={{1,0},{2,1},{3,2},{4,3},{5,4},{6,5},{7,6},{8,7},{9,8},{10,9},{11,1... | collective-permute-start | bytes 196616 | tf_op jit(solution)/shard_map/ppermute | solution.py:10
  221.4 0.6 iota_compare_fusion.3
  222.0 4.8 %collective-permute-done = bf16[2,2,32,256]{3,2,1,0:T(8,128)(2,1)S(1)} collective-permute-done((bf16[2,2,32,256]{3,2,1,0:T(8,128)(2,1)}, bf16[2,2,32,256]{3,2,1,0:T(8,128)(2,1)S(1)}, u32[]{:S(2)}, u32[]{:S(2)}) %collective-permute-start) | collective-permute-done | bytes 65568 | tf_op jit(solution)/shard_map/ppermute | solution.py:10
  226.7 0.8 maximum_bitcast_fusion
  227.6 0.1 copy.20
  227.7 0.1 reshape.27
  227.8 0.4 convolution_bitcast_fusion
  228.3 1.4 fusion.11
  229.7 2.1 fusion.3
  (9 shorter events, 0.2 us)
Async XLA Ops:
  6.5 211.7 %reduce-scatter.2.cloned.1.call-start = ((), (), s32[]{:S(2)}) async-start(), calls=%async_computation.2 | async-start | bytes 2162688 | tf_op jit(solution)/shard_map/reduce_scatter | solution.py:66
  115.8 0.7 copy-start.2
  115.8 6.0 %copy-start = (bf16[2,256]{1,0:T(2,128)(2,1)S(1)}, bf16[2,256]{1,0:T(2,128)(2,1)}, u32[]{:S(2)}) copy-start(bf16[2,256]{1,0:T(2,128)(2,1)} %param.11) | copy-start | bytes 3076
  116.4 7.8 %copy-start.1 = (f32[2,2]{1,0:T(2,128)S(1)}, f32[2,2]{1,0:T(2,128)}, u32[]{:S(2)}) copy-start(f32[2,2]{1,0:T(2,128)} %param.12) | copy-start | bytes 52
  218.3 8.5 %collective-permute-start = (bf16[2,2,32,256]{3,2,1,0:T(8,128)(2,1)}, bf16[2,2,32,256]{3,2,1,0:T(8,128)(2,1)S(1)}, u32[]{:S(2)}, u32[]{:S(2)}) collective-permute-start(bf16[2,2,32,256]{3,2,1,0:T(8,128)(2,1)} %reduce-scatter.2.cloned.1.call-done), channel_id=1, source_target_pairs={{1,0},{2,1},{3,2},{4,3},{5,4},{6,5},{7,6},{8,7},{9,8},{10,9},{11,1... | collective-permute-start | bytes 196616 | tf_op jit(solution)/shard_map/ppermute | solution.py:10
Sparse Core Ops, SparseCore 0:
  115.9 102.3 reduce-scatter.1
where the time goes:
time: 240 us; the launch traced here: 239 us
  waiting for transfers between devices  98 us (41%)
  blocking collectives  56.1 us (23%)
  local copies, waits for them, and re-layouts  51.2 us (21%)
  between operations  18.4 us (8%)
  matrix products  6.04 us (3%)
  other arithmetic  5.71 us (2%)
  starting transfers between devices  3.13 us (1%)
    reduce_scatter x1, waiting for transfers between devices, on_device(): lax.psum_scatter(regrouped.astype(jnp.float32).astype(jnp.bfloat16), 'ele...  93.2 us
    all_to_all x1, blocking collectives, on_device(): lax.all_to_all(partial_terms, 'range', split_axis=3, concat_axis=2, tiled...  56.1 us
    unnamed x9, local copies, waits for them, and re-layouts  23 us
    all_to_all x2, local copies, waits for them, and re-layouts, on_device(): lax.all_to_all(partial_terms, 'range', split_axis=3, concat_axis=2, tiled...  11.4 us
    convert_element_type x1, local copies, waits for them, and re-layouts, on_device(): product.reshape(beam_count, 2, pulse_dev, gate_count).astype(jnp.bfloat16)  7.31 us
    dot_general x1, local copies, waits for them, and re-layouts, on_device(): product = jnp.dot(stacked, samples, preferred_element_type=jnp.float32)  6.42 us
  transfers between devices with their start and end apart: 2, of which 2 were waited for; matrix products, arithmetic and copies ran while one was open for 2% of the time, Pallas kernels for 0%

commit v1 on v0

v1 whole, which is shorter than its diff:
```python
import jax
import jax.numpy as jnp
from jax import lax
from jax.experimental import pallas as pl
from jax.experimental.pallas import tpu as pltpu
from jax.sharding import Mesh, PartitionSpec as P

bf16, f32, i32 = jnp.bfloat16, jnp.float32, jnp.int32
LANES = 128
PAIR = 8
VMEM_BYTES = 60 << 20
SMALL_VMEM_BYTES = 24 << 20
FIRST = (((0,), (0,)), ((), ()))
LAST = (((1,), (1,)), ((), ()))


def iota(shape, dim):
    return lax.broadcasted_iota(i32, shape, dim)


def one_hot(condition):
    return condition.astype(f32).astype(bf16)


def steering(core, table_ref, index_ref, rows):
    elems = table_ref.shape[2]
    beams = index_ref.shape[1]
    select = one_hot(index_ref[...] == iota((table_ref.shape[1], beams), 0))
    row = iota((rows, beams), 0)
    half = lax.div(row, rows // 2)
    within = lax.rem(row, rows // 2)
    owner = jnp.where(half == 1, core, 1 - core)
    beam = lax.div(within, PAIR) * 4 + owner * 2 + lax.div(lax.rem(within, PAIR), 4)
    pick = one_hot(beam == iota((rows, beams), 1))
    parts = []
    for part in range(2):
        chosen = lax.dot_general(select, table_ref[part], FIRST, preferred_element_type=f32)
        parts.append(jnp.dot(pick, chosen.astype(bf16), preferred_element_type=f32))
    imag = lax.rem(lax.div(iota((rows, elems), 0), 2), 2) == 1
    by_real = jnp.where(imag, parts[1], parts[0]).astype(bf16)
    by_imag = jnp.where(imag, parts[0], -parts[1]).astype(bf16)
    widen = one_hot(lax.div(iota((elems, 2 * elems), 1), 2) == iota((elems, 2 * elems), 0))
    same_pulse = lax.rem(iota((rows, 2 * elems), 0), 2) == lax.rem(iota((rows, 2 * elems), 1), 2)
    wide = [
        jnp.where(same_pulse, jnp.dot(m, widen, preferred_element_type=f32), 0.0).astype(bf16)
        for m in (by_real, by_imag)
    ]
    return jnp.concatenate(wide, 1)


def beamform_kernel(index_ref, echo_ref, table_ref, other_ref, own_ref, weight_ref):
    rows = weight_ref.shape[0]

    @pl.when(pl.program_id(0) == 0)
    def _():
        weight_ref[...] = steering(lax.axis_index("c"), table_ref, index_ref, rows)

    samples = echo_ref[...].reshape(-1, echo_ref.shape[3])
    partial = jnp.dot(weight_ref[...], samples, preferred_element_type=f32).astype(bf16)
    other_ref[...] = partial[: rows // 2]
    own_ref[...] = partial[rows // 2 :]


def beamform(echoes, steer_table, beam_index):
    steps = 2
    _, elems, pulses, gates = echoes.shape
    beams = beam_index.shape[0]
    rows = 2 * beams * pulses
    width = gates // steps
    return pl.pallas_call(
        beamform_kernel,
        grid=(steps,),
        in_specs=[
            pl.BlockSpec((1, beams), lambda i: (0, 0)),
            pl.BlockSpec((2, elems, pulses, width), lambda i: (0, 0, 0, i)),
            pl.BlockSpec(steer_table.shape, lambda i: (0, 0, 0)),
        ],
        out_specs=[pl.BlockSpec((rows // 2, width), lambda i: (0, i))] * 2,
        out_shape=[jax.ShapeDtypeStruct((rows // 2, gates), bf16)] * 2,
        scratch_shapes=[pltpu.VMEM((rows, 4 * elems), bf16)],
        compiler_params=pltpu.CompilerParams(vmem_limit_bytes=VMEM_BYTES),
    )(beam_index.reshape(1, beams), echoes, steer_table)


def compress_kernel(own_ref, came_ref, code_ref, out_ref, signal_ref, turned_ref):
    rows, gates = own_ref.shape
    taps = code_ref.shape[1]
    row, column = iota((rows, rows), 0), iota((rows, rows), 1)
    imag = lax.rem(lax.div(row, 2), 2) == 1
    turn = jnp.where(imag, -(column == row - 2).astype(f32), (column == row + 2).astype(f32)).astype(bf16)
    signal = (own_ref[...].astype(f32) + came_ref[...].astype(f32)).astype(bf16)
    signal_ref[:, :gates] = signal
    signal_ref[:, gates:] = jnp.zeros((rows, taps), bf16)
    turned_ref[:, :gates] = jnp.dot(turn, signal, preferred_element_type=f32).astype(bf16)
    turned_ref[:, gates:] = jnp.zeros((rows, taps), bf16)
    bands = []
    for part in range(2):
        code = code_ref[part : part + 1, :].astype(f32)
        code = jnp.concatenate([code, jnp.zeros_like(code)], 1)
        code = jnp.broadcast_to(code, (taps, 2 * taps))
        bands.append(pltpu.roll(code, 0, 1, stride=1, stride_axis=0).astype(bf16))
    for slab in range(gates // taps):
        here = slice(slab * taps, (slab + 2) * taps)
        total = lax.dot_general(signal_ref[:, here], bands[0], LAST, preferred_element_type=f32)
        total += lax.dot_general(turned_ref[:, here], bands[1], LAST, preferred_element_type=f32)
        total = total.reshape(rows // PAIR, PAIR, taps)
        total = jnp.concatenate([total[:, :, :LANES], total[:, :, LANES:]], 1)
        out_ref[:, slab] = total.astype(bf16)


def compress(own, came, pulse_code):
    rows, gates = own.shape
    taps = pulse_code.shape[1]
    return pl.pallas_call(
        compress_kernel,
        out_shape=jax.ShapeDtypeStruct((rows // PAIR, gates // taps, 2 * PAIR, LANES), bf16),
        scratch_shapes=[pltpu.VMEM((rows, gates + taps), bf16)] * 2,
        compiler_params=pltpu.CompilerParams(vmem_limit_bytes=SMALL_VMEM_BYTES),
    )(own, came, pulse_code)


def delayed(value, spacing):
    rolled = pltpu.roll(value, spacing, 0)
    return jnp.where(iota(value.shape, 0) >= spacing, rolled, 0.0)


def filter_kernel(taps_ref, dilation_ref, parts_ref, out_ref, sum_ref):
    count, pairs = parts_ref.shape[:2]
    planes = sum_ref.shape[0]
    for pair in range(pairs):
        total = parts_ref[0, pair].astype(f32)
        for source in range(1, count):
            total += parts_ref[source, pair].astype(f32)
        for side in range(2):
            for plane in range(planes):
                row = side * PAIR + 2 * plane
                sum_ref[plane, 2 * pair : 2 * pair + 2, side * LANES : (side + 1) * LANES] = total[row : row + 2]
    for plane in range(planes):
        value = sum_ref[plane]
        for section in range(2):
            spacing = dilation_ref[section]
            near = taps_ref[section, 0] * delayed(value, spacing)
            far = taps_ref[section, 1] * delayed(value, 2 * spacing)
            value = value - near - far
        out_ref[plane] = value


def clutter_filter(parts, clutter_taps, dilation):
    pulses = 2 * parts.shape[1]
    planes = PAIR // 2
    width = 2 * LANES
    scalar = pl.BlockSpec(memory_space=pltpu.SMEM)
    return pl.pallas_call(
        filter_kernel,
        in_specs=[scalar, scalar, pl.BlockSpec(memory_space=pltpu.VMEM)],
        out_shape=jax.ShapeDtypeStruct((planes, pulses, width), f32),
        scratch_shapes=[pltpu.VMEM((planes, pulses, width), f32)],
        compiler_params=pltpu.CompilerParams(vmem_limit_bytes=SMALL_VMEM_BYTES),
    )(clutter_taps, dilation, parts)


def on_device(echoes, steer_table, beam_index, pulse_code, clutter_taps, dilation):
    x_count, z_count = lax.axis_size("x"), lax.axis_size("z")
    slabs = lax.axis_size("y") * lax.axis_size("w")
    other, own = beamform(echoes, steer_table, beam_index)
    came = lax.ppermute(other, "c", [(0, 1), (1, 0)])
    blocks = compress(own, came, pulse_code)
    blocks = blocks.reshape(x_count, z_count * slabs, 2 * PAIR, LANES)
    blocks = lax.all_to_all(blocks, "x", 0, 0)
    blocks = jnp.sum(blocks.astype(f32), 0).astype(bf16)
    blocks = lax.all_to_all(blocks, ("z", "y", "w"), 0, 0)
    blocks = blocks.reshape(z_count, slabs, 2 * PAIR, LANES)
    planes = clutter_filter(blocks, clutter_taps, dilation)
    return planes.reshape(2, 2, planes.shape[1], planes.shape[2])


def solution(mesh):
    split = Mesh(mesh.devices.reshape(4, 4, 2, 8, 2), ("x", "z", "c", "y", "w"))
    elem, gates = ("x", "z", "c"), ("y", "w")
    return jax.shard_map(
        on_device,
        mesh=split,
        in_specs=(P(None, elem, gates, None), P(None, None, elem), P(), P(), P(), P()),
        out_specs=P(elem, None, None, gates),
        check_vma=False,
    )
```

time: 240 us -> 64.3 us (0.27)
  the two profiles are of different devices: /device:TPU:88 before, /device:TPU:8 now
where the time goes in v1:
time: 64.3 us; the launch traced here: 64.1 us
  blocking collectives  48.5 us (75%)
  Pallas kernels  9.15 us (14%)
  waiting for transfers between devices  2.84 us (4%)
  starting transfers between devices  2.05 us (3%)
  local copies, waits for them, and re-layouts  1.24 us (2%)
    all_to_all x1, blocking collectives, on_device(): blocks = lax.all_to_all(blocks, ('z', 'y', 'w'), 0, 0)  29.1 us
    all_to_all x1, blocking collectives, on_device(): blocks = lax.all_to_all(blocks, 'x', 0, 0)  19.5 us
    pallas_call x1, Pallas kernels, beamform(): pl.pallas_call(beamform_kernel, grid=(steps,), in_specs=[pl.BlockSpec((1,...  4.57 us
    pallas_call x1, Pallas kernels, compress(): pl.pallas_call(compress_kernel, out_shape=jax.ShapeDtypeStruct((rows // P...  3.18 us
    ppermute x1, waiting for transfers between devices, on_device(): came = lax.ppermute(other, 'c', [(0, 1), (1, 0)])  2.84 us
    ppermute x1, starting transfers between devices, on_device(): came = lax.ppermute(other, 'c', [(0, 1), (1, 0)])  2.05 us
    pallas_call x1, Pallas kernels, clutter_filter(): pl.pallas_call(filter_kernel, in_specs=[scalar, scalar, pl.BlockSpec(memo...  1.4 us
  transfers between devices with their start and end apart: 1, of which 1 were waited for; matrix products, arithmetic and copies ran while one was open for 0% of the time, Pallas kernels for 0%

profile of v1, /device:TPU:8, one launch (start us, length us, event | category | flops | bytes accessed | tf_op | source)
XLA Modules:
  0.0 64.1 jit_solution(1121310669586580241)
XLA Ops:
  0.0 0.0 copy-start.1
  0.0 4.6 %shard_map.64 = (bf16[128,4096]{1,0:T(8,128)(2,1)}, bf16[128,4096]{1,0:T(8,128)(2,1)}) custom-call(s32[1,64]{1,0:T(1,128)} %bitcast.6, bf16[2,128,2,4096]{3,2,1,0:T(2,128)(2,1)} %echo_ref.1, bf16[2,128,128]{2,1,0:T(8,128)(2,1)} %table_ref.1), custom_call_target="tpu_custom_call" | custom-call | tf_op jit(solution)/shard_map/pallas_call | solution.py:70
  4.6 0.0 copy-start.2
  4.6 0.0 copy-start.3
  4.6 2.0 %collective-permute-start = (bf16[128,4096]{1,0:T(8,128)(2,1)}, bf16[128,4096]{1,0:T(8,128)(2,1)S(1)}, u32[]{:S(2)}, u32[]{:S(2)}) collective-permute-start(bf16[128,4096]{1,0:T(8,128)(2,1)} %get-tuple-element.8), channel_id=1, source_target_pairs={{0,16},{16,0},{1,17},{17,1},{2,18},{18,2},{3,19},{19,3},{4,20},{20... | collective-permute-start | bytes 3145736 | tf_op jit(solution)/shard_map/ppermute | solution.py:166
  6.6 2.8 %collective-permute-done.came_ref = bf16[128,4096]{1,0:T(8,128)(2,1)S(1)} collective-permute-done((bf16[128,4096]{1,0:T(8,128)(2,1)}, bf16[128,4096]{1,0:T(8,128)(2,1)S(1)}, u32[]{:S(2)}, u32[]{:S(2)}) %collective-permute-start) | collective-permute-done | bytes 1048608 | tf_op jit(solution)/shard_map/ppermute | solution.py:166
  9.5 0.0 copy-done.1
  9.5 0.0 copy-start
  9.5 1.2 %copy-done = bf16[128,4096]{1,0:T(8,128)(2,1)S(1)} copy-done((bf16[128,4096]{1,0:T(8,128)(2,1)S(1)}, bf16[128,4096]{1,0:T(8,128)(2,1)}, u32[]{:S(2)}) %copy-start) | copy-done | bytes 1048600
  10.7 3.2 %shard_map.65 = bf16[16,16,16,128]{3,2,1,0:T(8,128)(2,1)S(1)} custom-call(bf16[128,4096]{1,0:T(8,128)(2,1)S(1)} %copy-done, bf16[128,4096]{1,0:T(8,128)(2,1)S(1)} %collective-permute-done.came_ref, bf16[2,256]{1,0:T(2,128)(2,1)S(1)} %copy-done.1), custom_call_target="tpu_custom_call" | custom-call | tf_op jit(solution)/shard_map/pallas_call | solution.py:114
  13.9 19.5 %all_to_all.10 = bf16[4,64,16,128]{3,2,1,0:T(8,128)(2,1)S(1)} all-to-all(bf16[4,64,16,128]{3,2,1,0:T(8,128)(2,1)S(1)} %bitcast.4), channel_id=1, replica_groups=mesh['x'=4,'z'=4,'c'=2,'y'=8,'w'=2] {'x'}, dimensions={0} | all-to-all | bytes 2097152 | tf_op jit(solution)/shard_map/all_to_all | solution.py:169
  33.4 0.3 reduce_sum.12
  33.6 29.1 %all_to_all.11 = bf16[64,16,128]{2,1,0:T(8,128)(2,1)S(1)} all-to-all(bf16[64,16,128]{2,1,0:T(8,128)(2,1)S(1)} %reduce_sum.12), channel_id=1, replica_groups=mesh['x'=4,'z'=4,'c'=2,'y'=8,'w'=2] {'z','y','w'}, dimensions={0} | all-to-all | bytes 524288 | tf_op jit(solution)/shard_map/all_to_all | solution.py:171
  62.7 0.0 copy-done.2
  62.7 0.0 copy-done.3
  62.7 1.4 %shard_map.66 = f32[4,32,256]{2,1,0:T(8,128)} custom-call(f32[2,2]{1,0:T(2,128)S(1)} %copy-done.2, s32[2]{0:T(128)S(1)} %copy-done.3, bf16[4,16,16,128]{3,2,1,0:T(8,128)(2,1)S(1)} %bitcast.5), custom_call_target="tpu_custom_call" | custom-call | tf_op jit(solution)/shard_map/pallas_call | solution.py:153
Async XLA Ops:
  0.0 9.5 %copy-start.1 = (bf16[2,256]{1,0:T(2,128)(2,1)S(1)}, bf16[2,256]{1,0:T(2,128)(2,1)}, u32[]{:S(2)}) copy-start(bf16[2,256]{1,0:T(2,128)(2,1)} %code_ref.1) | copy-start | bytes 3076
  4.6 58.1 %copy-start.2 = (f32[2,2]{1,0:T(2,128)S(1)}, f32[2,2]{1,0:T(2,128)}, u32[]{:S(2)}) copy-start(f32[2,2]{1,0:T(2,128)} %taps_ref.1) | copy-start | bytes 52
  4.6 58.1 %copy-start.3 = (s32[2]{0:T(128)S(1)}, s32[2]{0:T(128)}, u32[]{:S(2)}) copy-start(s32[2]{0:T(128)} %dilation_ref.1) | copy-start | bytes 28
  4.6 4.9 %collective-permute-start = (bf16[128,4096]{1,0:T(8,128)(2,1)}, bf16[128,4096]{1,0:T(8,128)(2,1)S(1)}, u32[]{:S(2)}, u32[]{:S(2)}) collective-permute-start(bf16[128,4096]{1,0:T(8,128)(2,1)} %get-tuple-element.8), channel_id=1, source_target_pairs={{0,16},{16,0},{1,17},{17,1},{2,18},{18,2},{3,19},{19,3},{4,20},{20... | collective-permute-start | bytes 3145736 | tf_op jit(solution)/shard_map/ppermute | solution.py:166
  9.5 1.2 %copy-start = (bf16[128,4096]{1,0:T(8,128)(2,1)S(1)}, bf16[128,4096]{1,0:T(8,128)(2,1)}, u32[]{:S(2)}) copy-start(bf16[128,4096]{1,0:T(8,128)(2,1)} %get-tuple-element.7.own_ref) | copy-start | bytes 3145732

commit v2 on v1

v2 whole, which is shorter than its diff:
```python
import jax
import jax.numpy as jnp
from jax import lax
from jax.experimental import pallas as pl
from jax.experimental.pallas import tpu as pltpu
from jax.sharding import Mesh, PartitionSpec as P

bf16, f32, i32 = jnp.bfloat16, jnp.float32, jnp.int32
LANES = 128
PAIR = 8
VMEM_BYTES = 24 << 20
ECHO_STEPS = 4
FIRST = (((0,), (0,)), ((), ()))
LAST = (((1,), (1,)), ((), ()))


def iota(shape, dim):
    return lax.broadcasted_iota(i32, shape, dim)


def one_hot(condition):
    return condition.astype(f32).astype(bf16)


def steering(table_ref, index_ref, rows):
    core = lax.axis_index("c")
    elems = table_ref.shape[2]
    beams = index_ref.shape[1]
    select = one_hot(index_ref[...] == iota((table_ref.shape[1], beams), 0))
    row = iota((rows, beams), 0)
    half = lax.div(row, rows // 2)
    within = lax.rem(row, rows // 2)
    owner = jnp.where(half == 1, core, 1 - core)
    beam = lax.div(within, PAIR) * 4 + owner * 2 + lax.div(lax.rem(within, PAIR), 4)
    pick = one_hot(beam == iota((rows, beams), 1))
    parts = []
    for part in range(2):
        chosen = lax.dot_general(select, table_ref[part], FIRST, preferred_element_type=f32)
        parts.append(jnp.dot(pick, chosen.astype(bf16), preferred_element_type=f32))
    imag = lax.rem(lax.div(iota((rows, elems), 0), 2), 2) == 1
    by_real = jnp.where(imag, parts[1], parts[0]).astype(bf16)
    by_imag = jnp.where(imag, parts[0], -parts[1]).astype(bf16)
    widen = one_hot(lax.div(iota((elems, 2 * elems), 1), 2) == iota((elems, 2 * elems), 0))
    same_pulse = lax.rem(iota((rows, 2 * elems), 0), 2) == lax.rem(iota((rows, 2 * elems), 1), 2)
    wide = [
        jnp.where(same_pulse, jnp.dot(m, widen, preferred_element_type=f32), 0.0).astype(bf16)
        for m in (by_real, by_imag)
    ]
    return jnp.concatenate(wide, 1)


def beamform_kernel(index_hbm, table_hbm, echo_hbm, other_ref, own_ref, index_ref, table_ref, echo_ref, done):
    rows = 2 * other_ref.shape[0]
    pulses, gates = echo_hbm.shape[2:]
    width = gates // ECHO_STEPS
    small = [
        pltpu.make_async_copy(index_hbm, index_ref, done.at[ECHO_STEPS]),
        pltpu.make_async_copy(table_hbm, table_ref, done.at[ECHO_STEPS + 1]),
    ]
    spans = [slice(step * width, (step + 1) * width) for step in range(ECHO_STEPS)]
    large = [
        pltpu.make_async_copy(echo_hbm.at[:, :, :, span], echo_ref.at[:, :, :, span], done.at[step])
        for step, span in enumerate(spans)
    ]
    for copy in small + large:
        copy.start()
    for copy in small:
        copy.wait()
    weights = steering(table_ref, index_ref, rows)
    for span, copy in zip(spans, large):
        copy.wait()
        samples = echo_ref[:, :, :, span].reshape(-1, width)
        partial = jnp.dot(weights, samples, preferred_element_type=f32).astype(bf16)
        other_ref[:, span] = partial[: rows // 2]
        own_ref[:, span] = partial[rows // 2 :]


def beamform(echoes, steer_table, beam_index):
    _, elems, pulses, gates = echoes.shape
    beams = beam_index.shape[0]
    rows = 2 * beams * pulses
    operands = (beam_index.reshape(1, beams), steer_table, echoes)
    return pl.pallas_call(
        beamform_kernel,
        in_specs=[pl.BlockSpec(memory_space=pltpu.HBM)] * 3,
        out_specs=[pl.BlockSpec(memory_space=pltpu.VMEM)] * 2,
        out_shape=[jax.ShapeDtypeStruct((rows // 2, gates), bf16)] * 2,
        scratch_shapes=[
            pltpu.VMEM((1, beams), i32),
            pltpu.VMEM(steer_table.shape, bf16),
            pltpu.VMEM(echoes.shape, bf16),
            pltpu.SemaphoreType.DMA((ECHO_STEPS + 2,)),
        ],
        compiler_params=pltpu.CompilerParams(vmem_limit_bytes=VMEM_BYTES),
    )(*(pltpu.with_memory_space_constraint(a, pltpu.HBM) for a in operands))


def band_kernel(code_ref, band_ref):
    taps = code_ref.shape[1]
    for part in range(2):
        code = code_ref[part : part + 1, :].astype(f32)
        code = jnp.concatenate([code, jnp.zeros_like(code)], 1)
        code = jnp.broadcast_to(code, (taps, 2 * taps))
        band_ref[part] = pltpu.roll(code, 0, 1, stride=1, stride_axis=0).astype(bf16)


def toeplitz_bands(pulse_code):
    taps = pulse_code.shape[1]
    return pl.pallas_call(
        band_kernel,
        out_shape=jax.ShapeDtypeStruct((2, taps, 2 * taps), bf16),
        compiler_params=pltpu.CompilerParams(vmem_limit_bytes=VMEM_BYTES),
        cost_estimate=pl.CostEstimate(flops=1 << 22, bytes_accessed=1 << 22, transcendentals=0),
    )(pulse_code)


def compress_kernel(own_ref, came_ref, band_ref, out_ref):
    chunks, chips, slabs = out_ref.shape[:3]
    taps = band_ref.shape[1]
    rows = chips * PAIR
    past = jnp.zeros((rows, taps), bf16)
    for chunk in range(chunks):
        here = slice(chunk * rows, (chunk + 1) * rows)
        signal = own_ref[here].astype(f32) + came_ref[here].astype(f32)
        imag = lax.rem(lax.div(iota(signal.shape, 0), 2), 2) == 1
        turned = jnp.where(imag, -pltpu.roll(signal, 2, 0), pltpu.roll(signal, rows - 2, 0))
        total = None
        for part, values in enumerate((signal, turned)):
            values = jnp.concatenate([values.astype(bf16), past], 1)
            windows = [values[:, slab * taps : (slab + 2) * taps] for slab in range(slabs)]
            windows = jnp.concatenate(windows, 0)
            product = lax.dot_general(windows, band_ref[part], LAST, preferred_element_type=f32)
            total = product if total is None else total + product
        total = total.reshape(slabs, chips, PAIR, taps)
        for slab in range(slabs):
            block = total[slab]
            out_ref[chunk, :, slab] = jnp.concatenate([block[:, :, :LANES], block[:, :, LANES:]], 1).astype(bf16)


def compress(own, came, bands, chunks):
    rows, gates = own.shape
    taps = bands.shape[1]
    shape = (chunks, rows // PAIR // chunks, gates // taps, 2 * PAIR, LANES)
    return pl.pallas_call(
        compress_kernel,
        out_shape=jax.ShapeDtypeStruct(shape, bf16),
        compiler_params=pltpu.CompilerParams(vmem_limit_bytes=VMEM_BYTES),
    )(own, came, bands)


def sum_kernel(parts_ref, out_ref):
    total = parts_ref[0].astype(f32)
    for source in range(1, parts_ref.shape[0]):
        total += parts_ref[source].astype(f32)
    out_ref[...] = total.astype(bf16)


def summed(parts):
    return pl.pallas_call(
        sum_kernel,
        out_shape=jax.ShapeDtypeStruct(parts.shape[1:], bf16),
        compiler_params=pltpu.CompilerParams(vmem_limit_bytes=VMEM_BYTES),
    )(parts)


def delayed(value, spacing):
    rolled = pltpu.roll(value, spacing, 0)
    return jnp.where(iota(value.shape, 0) >= spacing, rolled, 0.0)


def filter_kernel(taps_ref, dilation_ref, parts_ref, out_ref, sum_ref):
    count, pairs = parts_ref.shape[:2]
    planes = sum_ref.shape[0]
    for pair in range(pairs):
        total = parts_ref[0, pair].astype(f32)
        for source in range(1, count):
            total += parts_ref[source, pair].astype(f32)
        for side in range(2):
            for plane in range(planes):
                row = side * PAIR + 2 * plane
                sum_ref[plane, 2 * pair : 2 * pair + 2, side * LANES : (side + 1) * LANES] = total[row : row + 2]
    for plane in range(planes):
        value = sum_ref[plane]
        for section in range(2):
            spacing = dilation_ref[section]
            near = taps_ref[section, 0] * delayed(value, spacing)
            far = taps_ref[section, 1] * delayed(value, 2 * spacing)
            value = value - near - far
        out_ref[plane] = value


def clutter_filter(parts, clutter_taps, dilation):
    pulses = 2 * parts.shape[1]
    planes = PAIR // 2
    width = 2 * LANES
    scalar = pl.BlockSpec(memory_space=pltpu.SMEM)
    return pl.pallas_call(
        filter_kernel,
        in_specs=[scalar, scalar, pl.BlockSpec(memory_space=pltpu.VMEM)],
        out_shape=jax.ShapeDtypeStruct((planes, pulses, width), f32),
        scratch_shapes=[pltpu.VMEM((planes, pulses, width), f32)],
        compiler_params=pltpu.CompilerParams(vmem_limit_bytes=VMEM_BYTES),
    )(clutter_taps, dilation, parts)


def on_device(echoes, steer_table, beam_index, pulse_code, clutter_taps, dilation):
    x_count, z_count = lax.axis_size("x"), lax.axis_size("z")
    slabs = lax.axis_size("y") * lax.axis_size("w")
    other, own = beamform(echoes, steer_table, beam_index)
    came = lax.ppermute(other, "c", [(0, 1), (1, 0)])
    bands = toeplitz_bands(pulse_code)
    blocks = compress(own, came, bands, x_count)
    blocks = summed(lax.all_to_all(blocks, "x", 0, 0)).reshape(z_count * slabs, 2 * PAIR, LANES)
    blocks = lax.all_to_all(blocks, ("z", "y", "w"), 0, 0)
    blocks = blocks.reshape(z_count, slabs, 2 * PAIR, LANES)
    planes = clutter_filter(blocks, clutter_taps, dilation)
    return planes.reshape(2, 2, planes.shape[1], planes.shape[2])


def solution(mesh):
    split = Mesh(mesh.devices.reshape(4, 4, 2, 8, 2), ("x", "z", "c", "y", "w"))
    elem, gates = ("x", "z", "c"), ("y", "w")
    return jax.shard_map(
        on_device,
        mesh=split,
        in_specs=(P(None, elem, gates, None), P(None, None, elem), P(), P(), P(), P()),
        out_specs=P(elem, None, None, gates),
        check_vma=False,
    )
```

time: 64.3 us -> 60.2 us (0.936)
  Pallas kernels: 9.15 us -> 6.96 us
  local copies, waits for them, and re-layouts: 1.24 us -> 0.02 us
    pallas_call x2 -> x4, Pallas kernels: 7.74 us -> 5.56 us  [the longest x1 3.68 us: beamform(): pl.pallas_call(beamform_kernel, in_specs=[pl.BlockSpec(memory_space=pltpu...]
    unnamed x8 -> x6, local copies, waits for them, and re-layouts: 1.24 us -> 0.02 us
where the time goes in v2:
time: 60.2 us; the launch traced here: 60 us
  blocking collectives  48.5 us (81%)
  Pallas kernels  6.96 us (12%)
  waiting for transfers between devices  2.48 us (4%)
  starting transfers between devices  1.92 us (3%)
    all_to_all x1, blocking collectives, on_device(): blocks = lax.all_to_all(blocks, ('z', 'y', 'w'), 0, 0)  29.1 us
    all_to_all x1, blocking collectives, on_device(): lax.all_to_all(blocks, 'x', 0, 0)  19.5 us
    pallas_call x1, Pallas kernels, beamform(): pl.pallas_call(beamform_kernel, in_specs=[pl.BlockSpec(memory_space=pltpu...  3.68 us
    ppermute x1, waiting for transfers between devices, on_device(): came = lax.ppermute(other, 'c', [(0, 1), (1, 0)])  2.48 us
    ppermute x1, starting transfers between devices, on_device(): came = lax.ppermute(other, 'c', [(0, 1), (1, 0)])  1.92 us
    pallas_call x1, Pallas kernels, compress(): pl.pallas_call(compress_kernel, out_shape=jax.ShapeDtypeStruct(shape, bf1...  1.63 us
    pallas_call x1, Pallas kernels, clutter_filter(): pl.pallas_call(filter_kernel, in_specs=[scalar, scalar, pl.BlockSpec(memo...  1.4 us
  transfers between devices with their start and end apart: 1, of which 1 were waited for; matrix products, arithmetic and copies ran while one was open for 0% of the time, Pallas kernels for 0%

profile of v2, /device:TPU:8, one launch (start us, length us, event | category | flops | bytes accessed | tf_op | source)
XLA Modules:
  0.0 60.0 jit_solution(6190568503047227177)
XLA Ops:
  0.0 0.0 copy-start
  0.0 3.7 %shard_map.64 = (bf16[128,4096]{1,0:T(8,128)(2,1)S(1)}, bf16[128,4096]{1,0:T(8,128)(2,1)S(1)}) custom-call(s32[1,64]{1,0:T(1,128)} %bitcast.6, bf16[2,128,128]{2,1,0:T(8,128)(2,1)} %table_hbm.1, bf16[2,128,2,4096]{3,2,1,0:T(2,128)(2,1)} %echo_hbm.1), custom_call_target="tpu_custom_call" | custom-call | tf_op jit(solution)/shard_map/pallas_call | solution.py:83
  3.7 0.0 copy-start.1
  3.7 0.0 copy-start.2
  3.7 1.9 %collective-permute-start = (bf16[128,4096]{1,0:T(8,128)(2,1)S(1)}, bf16[128,4096]{1,0:T(8,128)(2,1)S(1)}, u32[]{:S(2)}, u32[]{:S(2)}) collective-permute-start(bf16[128,4096]{1,0:T(8,128)(2,1)S(1)} %get-tuple-element.8), channel_id=1, source_target_pairs={{0,16},{16,0},{1,17},{17,1},{2,18},{18,2},{3,19},{19,3},{4,20},{20... | collective-permute-start | bytes 3145736 | tf_op jit(solution)/shard_map/ppermute | solution.py:210
  5.6 0.0 copy-done
  5.6 0.1 shard_map.65.band_ref
  5.8 2.5 %collective-permute-done.came_ref = bf16[128,4096]{1,0:T(8,128)(2,1)S(1)} collective-permute-done((bf16[128,4096]{1,0:T(8,128)(2,1)S(1)}, bf16[128,4096]{1,0:T(8,128)(2,1)S(1)}, u32[]{:S(2)}, u32[]{:S(2)}) %collective-permute-start) | collective-permute-done | bytes 1048608 | tf_op jit(solution)/shard_map/ppermute | solution.py:210
  8.3 1.6 %shard_map.66 = bf16[4,4,16,16,128]{4,3,2,1,0:T(8,128)(2,1)S(1)} custom-call(bf16[128,4096]{1,0:T(8,128)(2,1)S(1)} %get-tuple-element.7.own_ref, bf16[128,4096]{1,0:T(8,128)(2,1)S(1)} %collective-permute-done.came_ref, bf16[2,256,512]{2,1,0:T(8,128)(2,1)S(1)} %shard_map.65.band_ref), custom_call_target="tpu_custom_call" | custom-call | tf_op jit(solution)/shard_map/pallas_call | solution.py:144
  9.9 19.5 %all_to_all.10.parts_ref = bf16[4,4,16,16,128]{4,3,2,1,0:T(8,128)(2,1)S(1)} all-to-all(bf16[4,4,16,16,128]{4,3,2,1,0:T(8,128)(2,1)S(1)} %shard_map.66), channel_id=1, replica_groups=mesh['x'=4,'z'=4,'c'=2,'y'=8,'w'=2] {'x'}, dimensions={0} | all-to-all | bytes 2097152 | tf_op jit(solution)/shard_map/all_to_all | solution.py:213
  29.4 0.1 shard_map.67
  29.5 29.1 %all_to_all.11 = bf16[64,16,128]{2,1,0:T(8,128)(2,1)S(1)} all-to-all(bf16[64,16,128]{2,1,0:T(8,128)(2,1)S(1)} %bitcast.4), channel_id=1, replica_groups=mesh['x'=4,'z'=4,'c'=2,'y'=8,'w'=2] {'z','y','w'}, dimensions={0} | all-to-all | bytes 524288 | tf_op jit(solution)/shard_map/all_to_all | solution.py:214
  58.6 0.0 copy-done.1
  58.6 0.0 copy-done.2
  58.6 1.4 %shard_map.68 = f32[4,32,256]{2,1,0:T(8,128)} custom-call(f32[2,2]{1,0:T(2,128)S(1)} %copy-done.1, s32[2]{0:T(128)S(1)} %copy-done.2, bf16[4,16,16,128]{3,2,1,0:T(8,128)(2,1)S(1)} %bitcast.5), custom_call_target="tpu_custom_call" | custom-call | tf_op jit(solution)/shard_map/pallas_call | solution.py:197
Async XLA Ops:
  0.0 5.6 %copy-start = (bf16[2,256]{1,0:T(2,128)(2,1)S(1)}, bf16[2,256]{1,0:T(2,128)(2,1)}, u32[]{:S(2)}) copy-start(bf16[2,256]{1,0:T(2,128)(2,1)} %code_ref.1) | copy-start | bytes 3076
  3.7 54.9 %copy-start.1 = (f32[2,2]{1,0:T(2,128)S(1)}, f32[2,2]{1,0:T(2,128)}, u32[]{:S(2)}) copy-start(f32[2,2]{1,0:T(2,128)} %taps_ref.1) | copy-start | bytes 52
  3.7 54.9 %copy-start.2 = (s32[2]{0:T(128)S(1)}, s32[2]{0:T(128)}, u32[]{:S(2)}) copy-start(s32[2]{0:T(128)} %dilation_ref.1) | copy-start | bytes 28
  3.7 4.6 %collective-permute-start = (bf16[128,4096]{1,0:T(8,128)(2,1)S(1)}, bf16[128,4096]{1,0:T(8,128)(2,1)S(1)}, u32[]{:S(2)}, u32[]{:S(2)}) collective-permute-start(bf16[128,4096]{1,0:T(8,128)(2,1)S(1)} %get-tuple-element.8), channel_id=1, source_target_pairs={{0,16},{16,0},{1,17},{17,1},{2,18},{18,2},{3,19},{19,3},{4,20},{20... | collective-permute-start | bytes 3145736 | tf_op jit(solution)/shard_map/ppermute | solution.py:210

commit v3 on v2

v3 whole, which is shorter than its diff:
```python
import jax
import jax.numpy as jnp
from jax import lax
from jax.experimental import pallas as pl
from jax.experimental.pallas import tpu as pltpu
from jax.sharding import Mesh, PartitionSpec as P

bf16, f32, i32 = jnp.bfloat16, jnp.float32, jnp.int32
LANES = 128
PAIR = 8
VMEM_BYTES = 24 << 20
ECHO_STEPS = 2
FIRST = (((0,), (0,)), ((), ()))
LAST = (((1,), (1,)), ((), ()))


def iota(shape, dim):
    return lax.broadcasted_iota(i32, shape, dim)


def one_hot(condition):
    return condition.astype(f32).astype(bf16)


def steering(table_ref, index_ref, rows, core):
    elems = table_ref.shape[2]
    beams = index_ref.shape[1]
    select = one_hot(index_ref[...] == iota((table_ref.shape[1], beams), 0))
    row = iota((rows, beams), 0)
    beam = lax.div(row, PAIR) * 4 + core * 2 + lax.rem(lax.div(row, 2), 2)
    pick = one_hot(beam == iota((rows, beams), 1))
    parts = []
    for part in range(2):
        chosen = lax.dot_general(select, table_ref[part], FIRST, preferred_element_type=f32)
        parts.append(jnp.dot(pick, chosen.astype(bf16), preferred_element_type=f32))
    imag = lax.rem(iota((rows, elems), 0), 2) == 1
    by_real = jnp.where(imag, parts[1], parts[0]).astype(bf16)
    by_imag = jnp.where(imag, parts[0], -parts[1]).astype(bf16)
    widen = one_hot(lax.div(iota((elems, 2 * elems), 1), 2) == iota((elems, 2 * elems), 0))
    same_pulse = lax.div(lax.rem(iota((rows, 2 * elems), 0), PAIR), 4) == lax.rem(iota((rows, 2 * elems), 1), 2)
    wide = [
        jnp.where(same_pulse, jnp.dot(m, widen, preferred_element_type=f32), 0.0).astype(bf16)
        for m in (by_real, by_imag)
    ]
    return jnp.concatenate(wide, 1)


def beam_chunk(weights, echo_ref, span):
    samples = echo_ref[:, :, :, span].reshape(weights.shape[1], -1)
    return jnp.dot(weights, samples, preferred_element_type=f32).astype(bf16)


def other_kernel(index_hbm, table_hbm, echo_hbm, other_ref, index_ref, table_ref, echo_ref, done):
    gates = echo_hbm.shape[3]
    width = gates // ECHO_STEPS
    small = [
        pltpu.make_async_copy(index_hbm, index_ref, done.at[ECHO_STEPS]),
        pltpu.make_async_copy(table_hbm, table_ref, done.at[ECHO_STEPS + 1]),
    ]
    spans = [slice(step * width, (step + 1) * width) for step in range(ECHO_STEPS)]
    large = [
        pltpu.make_async_copy(echo_hbm.at[:, :, :, span], echo_ref.at[:, :, :, span], done.at[step])
        for step, span in enumerate(spans)
    ]
    for copy in small + large:
        copy.start()
    for copy in small:
        copy.wait()
    weights = steering(table_ref, index_ref, other_ref.shape[0], 1 - lax.axis_index("c"))
    for span, copy in zip(spans, large):
        copy.wait()
        other_ref[:, span] = beam_chunk(weights, echo_ref, span)


def own_kernel(index_ref, table_ref, echo_ref, own_ref):
    gates = own_ref.shape[1]
    width = gates // ECHO_STEPS
    weights = steering(table_ref, index_ref, own_ref.shape[0], lax.axis_index("c"))
    for step in range(ECHO_STEPS):
        span = slice(step * width, (step + 1) * width)
        own_ref[:, span] = beam_chunk(weights, echo_ref, span)


def beamform(echoes, steer_table, beam_index):
    _, _, pulses, gates = echoes.shape
    beams = beam_index.shape[0]
    partial = jax.ShapeDtypeStruct((beams * pulses, gates), bf16)
    operands = (beam_index.reshape(1, beams), steer_table, echoes)
    near = pl.BlockSpec(memory_space=pltpu.VMEM)
    other, *held = pl.pallas_call(
        other_kernel,
        in_specs=[pl.BlockSpec(memory_space=pltpu.HBM)] * 3,
        out_specs=[near] * 4,
        out_shape=[partial] + [jax.ShapeDtypeStruct(a.shape, a.dtype) for a in operands],
        scratch_shapes=[pltpu.SemaphoreType.DMA((ECHO_STEPS + 2,))],
        compiler_params=pltpu.CompilerParams(vmem_limit_bytes=VMEM_BYTES),
    )(*(pltpu.with_memory_space_constraint(a, pltpu.HBM) for a in operands))

    def own():
        return pl.pallas_call(
            own_kernel,
            in_specs=[near] * 3,
            out_specs=near,
            out_shape=partial,
            compiler_params=pltpu.CompilerParams(vmem_limit_bytes=VMEM_BYTES),
            cost_estimate=pl.CostEstimate(flops=1 << 30, bytes_accessed=1 << 22, transcendentals=0),
        )(*held)

    return other, own


def band_kernel(code_ref, band_ref):
    taps = code_ref.shape[1]
    for part in range(2):
        code = code_ref[part : part + 1, :].astype(f32)
        code = jnp.concatenate([code, jnp.zeros_like(code)], 1)
        code = jnp.broadcast_to(code, (taps, 2 * taps))
        band_ref[part] = pltpu.roll(code, 0, 1, stride=1, stride_axis=0).astype(bf16)


def toeplitz_bands(pulse_code):
    taps = pulse_code.shape[1]
    return pl.pallas_call(
        band_kernel,
        out_shape=jax.ShapeDtypeStruct((2, taps, 2 * taps), bf16),
        compiler_params=pltpu.CompilerParams(vmem_limit_bytes=VMEM_BYTES),
        cost_estimate=pl.CostEstimate(flops=1 << 22, bytes_accessed=1 << 22, transcendentals=0),
    )(pulse_code)


def add_kernel(own_ref, came_ref, out_ref):
    rows = out_ref.shape[1]
    for chunk in range(out_ref.shape[0]):
        here = slice(chunk * rows, (chunk + 1) * rows)
        out_ref[chunk] = (own_ref[here].astype(f32) + came_ref[here].astype(f32)).astype(bf16)


def added(own, came, chunks):
    rows, gates = own.shape
    return pl.pallas_call(
        add_kernel,
        out_shape=jax.ShapeDtypeStruct((chunks, rows // chunks, gates), bf16),
        compiler_params=pltpu.CompilerParams(vmem_limit_bytes=VMEM_BYTES),
    )(own, came)


def compress_kernel(parts_ref, band_ref, out_ref):
    sources, rows, _ = parts_ref.shape
    chips, slabs = out_ref.shape[:2]
    taps = band_ref.shape[1]
    signal = parts_ref[0].astype(f32)
    for source in range(1, sources):
        signal += parts_ref[source].astype(f32)
    imag = lax.rem(iota(signal.shape, 0), 2) == 1
    turned = jnp.where(imag, -pltpu.roll(signal, 1, 0), pltpu.roll(signal, rows - 1, 0))
    past = jnp.zeros((rows, taps), bf16)
    total = None
    for part, values in enumerate((signal, turned)):
        values = jnp.concatenate([values.astype(bf16), past], 1)
        windows = [values[:, slab * taps : (slab + 2) * taps] for slab in range(slabs)]
        windows = jnp.concatenate(windows, 0)
        product = lax.dot_general(windows, band_ref[part], LAST, preferred_element_type=f32)
        total = product if total is None else total + product
    total = total.reshape(slabs, chips, PAIR, taps)
    for slab in range(slabs):
        block = total[slab]
        out_ref[:, slab] = jnp.concatenate([block[:, :, :LANES], block[:, :, LANES:]], 1).astype(bf16)


def compress(parts, bands):
    _, rows, gates = parts.shape
    taps = bands.shape[1]
    return pl.pallas_call(
        compress_kernel,
        out_shape=jax.ShapeDtypeStruct((rows // PAIR, gates // taps, 2 * PAIR, LANES), bf16),
        compiler_params=pltpu.CompilerParams(vmem_limit_bytes=VMEM_BYTES),
    )(parts, bands)


def delays(value, spacing):
    rows, width = value.shape
    planes = PAIR // 2
    zeros = jnp.zeros((PAIR, width), f32)
    padded = jnp.concatenate([zeros, zeros, zeros, value], 0)
    turned = pltpu.roll(padded, planes, 0)

    def late(pulses):
        source, first = (padded, 3 * PAIR - pulses * planes) if pulses % 2 == 0 else (turned, 3 * PAIR - (pulses - 1) * planes)
        return source[first : first + rows]

    near = jnp.where(spacing == 1, late(1), jnp.where(spacing == 2, late(2), late(3)))
    far = jnp.where(spacing == 1, late(2), jnp.where(spacing == 2, late(4), late(6)))
    return near, far


def filter_kernel(taps_ref, dilation_ref, parts_ref, out_ref, value_ref):
    count, pairs = parts_ref.shape[:2]
    planes, pulses = out_ref.shape[:2]
    total = parts_ref[0].astype(f32)
    for source in range(1, count):
        total += parts_ref[source].astype(f32)
    for side in range(2):
        value = total[:, side * PAIR : (side + 1) * PAIR].reshape(pairs * PAIR, LANES)
        for section in range(2):
            near, far = delays(value, dilation_ref[section])
            value = value - taps_ref[section, 0] * near - taps_ref[section, 1] * far
        value_ref[...] = value
        for plane in range(planes):
            out_ref[plane, :, side * LANES : (side + 1) * LANES] = value_ref[pl.ds(plane, pulses, stride=planes), :]


def clutter_filter(parts, clutter_taps, dilation):
    pulses = 2 * parts.shape[1]
    planes = PAIR // 2
    scalar = pl.BlockSpec(memory_space=pltpu.SMEM)
    return pl.pallas_call(
        filter_kernel,
        in_specs=[scalar, scalar, pl.BlockSpec(memory_space=pltpu.VMEM)],
        out_shape=jax.ShapeDtypeStruct((planes, pulses, 2 * LANES), f32),
        scratch_shapes=[pltpu.VMEM((pulses * planes, LANES), f32)],
        compiler_params=pltpu.CompilerParams(vmem_limit_bytes=VMEM_BYTES),
    )(clutter_taps, dilation, parts)


def on_device(echoes, steer_table, beam_index, pulse_code, clutter_taps, dilation):
    x_count, z_count = lax.axis_size("x"), lax.axis_size("z")
    slabs = lax.axis_size("y") * lax.axis_size("w")
    other, own = beamform(echoes, steer_table, beam_index)
    came = lax.ppermute(other, "c", [(0, 1), (1, 0)])
    own = own()
    bands = toeplitz_bands(pulse_code)
    came, bands = lax.optimization_barrier((came, bands))
    parts = lax.all_to_all(added(own, came, x_count), "x", 0, 0)
    blocks = compress(parts, bands).reshape(z_count * slabs, 2 * PAIR, LANES)
    blocks = lax.all_to_all(blocks, ("z", "y", "w"), 0, 0)
    blocks = blocks.reshape(z_count, slabs, 2 * PAIR, LANES)
    planes = clutter_filter(blocks, clutter_taps, dilation)
    return planes.reshape(2, 2, planes.shape[1], planes.shape[2])


def solution(mesh):
    split = Mesh(mesh.devices.reshape(4, 4, 2, 8, 2), ("x", "z", "c", "y", "w"))
    elem, gates = ("x", "z", "c"), ("y", "w")
    return jax.shard_map(
        on_device,
        mesh=split,
        in_specs=(P(None, elem, gates, None), P(None, None, elem), P(), P(), P(), P()),
        out_specs=P(elem, None, None, gates),
        check_vma=False,
    )
```

time: 60.2 us -> 58.8 us (0.977)
  waiting for transfers between devices: 2.48 us -> 0.5 us
  Pallas kernels: 6.96 us -> 7.58 us
    ppermute x1, waiting for transfers between devices: 2.48 us -> 0.5 us  [on_device(): came = lax.ppermute(other, 'c', [(0, 1), (1, 0)])]
    pallas_call x3 -> x4, Pallas kernels: 5.43 us -> 6.12 us  [the longest x1 3.36 us: beamform(): pl.pallas_call(other_kernel, in_specs=[pl.BlockSpec(memory_space=pltpu.HB...]
  transfers between devices with their start and end apart: 1 -> 1, of which waited for: 1 -> 1; matrix products, arithmetic and copies ran while one was open for 0% -> 0% of each run, Pallas kernels for 0% -> 4%
where the time goes in v3:
time: 58.8 us; the launch traced here: 58.6 us
  blocking collectives  48.5 us (82%)
  Pallas kernels  7.58 us (13%)
  starting transfers between devices  1.92 us (3%)
    all_to_all x1, blocking collectives, on_device(): blocks = lax.all_to_all(blocks, ('z', 'y', 'w'), 0, 0)  29.1 us
    all_to_all x1, blocking collectives, on_device(): parts = lax.all_to_all(added(own, came, x_count), 'x', 0, 0)  19.5 us
    pallas_call x1, Pallas kernels, beamform(): pl.pallas_call(other_kernel, in_specs=[pl.BlockSpec(memory_space=pltpu.HB...  3.36 us
    pallas_call x1, Pallas kernels, own(): pl.pallas_call(own_kernel, in_specs=[near] * 3, out_specs=near, out_shape...  1.95 us
    ppermute x1, starting transfers between devices, on_device(): came = lax.ppermute(other, 'c', [(0, 1), (1, 0)])  1.92 us
    pallas_call x1, Pallas kernels, clutter_filter(): pl.pallas_call(filter_kernel, in_specs=[scalar, scalar, pl.BlockSpec(memo...  1.34 us
  transfers between devices with their start and end apart: 1, of which 1 were waited for; matrix products, arithmetic and copies ran while one was open for 0% of the time, Pallas kernels for 4%

profile of v3, /device:TPU:8, one launch (start us, length us, event | category | flops | bytes accessed | tf_op | source)
XLA Modules:
  0.0 58.6 jit_solution(8171399687244653534)
XLA Ops:
  0.0 0.0 copy-start
  0.0 3.4 %shard_map.64 = (bf16[128,4096]{1,0:T(8,128)(2,1)S(1)}, s32[1,64]{1,0:T(1,128)S(1)}, bf16[2,128,128]{2,1,0:T(8,128)(2,1)S(1)}, bf16[2,128,2,4096]{3,2,1,0:T(2,128)(2,1)S(1)}) custom-call(s32[1,64]{1,0:T(1,128)} %bitcast.6, bf16[2,128,128]{2,1,0:T(8,128)(2,1)} %table_hbm.1, bf16[2,128,2,4096]{3,2,1,0:T(2,128)(2,1)} %echo_hbm.1), custom_call_target="tpu_custom_call" | custom-call | tf_op jit(solution)/shard_map/pallas_call | solution.py:90
  3.4 1.9 %collective-permute-start = (bf16[128,4096]{1,0:T(8,128)(2,1)S(1)}, bf16[128,4096]{1,0:T(8,128)(2,1)S(1)}, u32[]{:S(2)}, u32[]{:S(2)}) collective-permute-start(bf16[128,4096]{1,0:T(8,128)(2,1)S(1)} %get-tuple-element.14), channel_id=1, source_target_pairs={{0,16},{16,0},{1,17},{17,1},{2,18},{18,2},{3,19},{19,3},{4,20},{20... | collective-permute-start | bytes 3145736 | tf_op jit(solution)/shard_map/ppermute | solution.py:229
  5.3 0.0 copy-done
  5.3 0.1 shard_map.66.band_ref
  5.4 2.0 %shard_map.65.own_ref = bf16[128,4096]{1,0:T(8,128)(2,1)S(1)} custom-call(s32[1,64]{1,0:T(1,128)S(1)} %get-tuple-element.11.index_ref, bf16[2,128,128]{2,1,0:T(8,128)(2,1)S(1)} %get-tuple-element.12.table_ref, bf16[2,128,2,4096]{3,2,1,0:T(2,128)(2,1)S(1)} %get-tuple-element.13.echo_ref), custom_call_target="tpu_custom_call" | custom-call | flops 1073741824 | bytes 4194304 | tf_op jit(solution)/shard_map/pallas_call | solution.py:100
  7.4 0.0 copy-start.1
  7.4 0.0 copy-start.2
  7.4 0.5 collective-permute-done.came_ref
  7.9 0.3 shard_map.67
  8.2 19.5 %all_to_all.10.parts_ref = bf16[4,32,4096]{2,1,0:T(8,128)(2,1)S(1)} all-to-all(bf16[4,32,4096]{2,1,0:T(8,128)(2,1)S(1)} %shard_map.67), channel_id=1, replica_groups=mesh['x'=4,'z'=4,'c'=2,'y'=8,'w'=2] {'x'}, dimensions={0} | all-to-all | bytes 2097152 | tf_op jit(solution)/shard_map/all_to_all | solution.py:233
  27.7 0.5 shard_map.68
  28.2 29.1 %all_to_all.11 = bf16[64,16,128]{2,1,0:T(8,128)(2,1)S(1)} all-to-all(bf16[64,16,128]{2,1,0:T(8,128)(2,1)S(1)} %bitcast.4), channel_id=1, replica_groups=mesh['x'=4,'z'=4,'c'=2,'y'=8,'w'=2] {'z','y','w'}, dimensions={0} | all-to-all | bytes 524288 | tf_op jit(solution)/shard_map/all_to_all | solution.py:235
  57.3 0.0 copy-done.1
  57.3 0.0 copy-done.2
  57.3 1.3 %shard_map.69 = f32[4,32,256]{2,1,0:T(8,128)} custom-call(f32[2,2]{1,0:T(2,128)S(1)} %copy-done.1, s32[2]{0:T(128)S(1)} %copy-done.2, bf16[4,16,16,128]{3,2,1,0:T(8,128)(2,1)S(1)} %bitcast.5), custom_call_target="tpu_custom_call" | custom-call | tf_op jit(solution)/shard_map/pallas_call | solution.py:216
Async XLA Ops:
  0.0 5.3 %copy-start = (bf16[2,256]{1,0:T(2,128)(2,1)S(1)}, bf16[2,256]{1,0:T(2,128)(2,1)}, u32[]{:S(2)}) copy-start(bf16[2,256]{1,0:T(2,128)(2,1)} %code_ref.1) | copy-start | bytes 3076
  3.4 4.6 %collective-permute-start = (bf16[128,4096]{1,0:T(8,128)(2,1)S(1)}, bf16[128,4096]{1,0:T(8,128)(2,1)S(1)}, u32[]{:S(2)}, u32[]{:S(2)}) collective-permute-start(bf16[128,4096]{1,0:T(8,128)(2,1)S(1)} %get-tuple-element.14), channel_id=1, source_target_pairs={{0,16},{16,0},{1,17},{17,1},{2,18},{18,2},{3,19},{19,3},{4,20},{20... | collective-permute-start | bytes 3145736 | tf_op jit(solution)/shard_map/ppermute | solution.py:229
  7.4 49.9 %copy-start.1 = (f32[2,2]{1,0:T(2,128)S(1)}, f32[2,2]{1,0:T(2,128)}, u32[]{:S(2)}) copy-start(f32[2,2]{1,0:T(2,128)} %taps_ref.1) | copy-start | bytes 52
  7.4 49.9 %copy-start.2 = (s32[2]{0:T(128)S(1)}, s32[2]{0:T(128)}, u32[]{:S(2)}) copy-start(s32[2]{0:T(128)} %dilation_ref.1) | copy-start | bytes 28

commit v4 on v3

--- a/solution.py
+++ b/solution.py
@@ -196,14 +196,17 @@
 def filter_kernel(taps_ref, dilation_ref, parts_ref, out_ref, value_ref):
     count, pairs = parts_ref.shape[:2]
     planes, pulses = out_ref.shape[:2]
-    total = parts_ref[0].astype(f32)
-    for source in range(1, count):
-        total += parts_ref[source].astype(f32)
+    rows = pairs * PAIR
     for side in range(2):
-        value = total[:, side * PAIR : (side + 1) * PAIR].reshape(pairs * PAIR, LANES)
+        here = slice(side * PAIR, (side + 1) * PAIR)
+        total = parts_ref[0, :, here].astype(f32)
+        for source in range(1, count):
+            total += parts_ref[source, :, here].astype(f32)
+        value = total.reshape(rows, LANES)
         for section in range(2):
-            near, far = delays(value, dilation_ref[section])
-            value = value - taps_ref[section, 0] * near - taps_ref[section, 1] * far
+            spacing = jnp.broadcast_to(dilation_ref[:, section : section + 1], value.shape)
+            near, far = delays(value, spacing)
+            value = value - taps_ref[section : section + 1, 0:1] * near - taps_ref[section : section + 1, 1:2] * far
         value_ref[...] = value
         for plane in range(planes):
             out_ref[plane, :, side * LANES : (side + 1) * LANES] = value_ref[pl.ds(plane, pulses, stride=planes), :]
@@ -212,14 +215,14 @@
 def clutter_filter(parts, clutter_taps, dilation):
     pulses = 2 * parts.shape[1]
     planes = PAIR // 2
-    scalar = pl.BlockSpec(memory_space=pltpu.SMEM)
+    near = pl.BlockSpec(memory_space=pltpu.VMEM)
     return pl.pallas_call(
         filter_kernel,
-        in_specs=[scalar, scalar, pl.BlockSpec(memory_space=pltpu.VMEM)],
+        in_specs=[near] * 3,
         out_shape=jax.ShapeDtypeStruct((planes, pulses, 2 * LANES), f32),
         scratch_shapes=[pltpu.VMEM((pulses * planes, LANES), f32)],
         compiler_params=pltpu.CompilerParams(vmem_limit_bytes=VMEM_BYTES),
-    )(clutter_taps, dilation, parts)
+    )(clutter_taps, dilation.reshape(1, -1), parts)
 
 
 def on_device(echoes, steer_table, beam_index, pulse_code, clutter_taps, dilation):

time: 58.8 us -> 58.3 us (level)
  no operation moved by 1% of the time
where the time goes in v4:
time: 58.3 us; the launch traced here: 58.1 us
  blocking collectives  48.5 us (83%)
  Pallas kernels  7.08 us (12%)
  starting transfers between devices  1.92 us (3%)
    all_to_all x1, blocking collectives, on_device(): blocks = lax.all_to_all(blocks, ('z', 'y', 'w'), 0, 0)  29.1 us
    all_to_all x1, blocking collectives, on_device(): parts = lax.all_to_all(added(own, came, x_count), 'x', 0, 0)  19.5 us
    pallas_call x1, Pallas kernels, beamform(): pl.pallas_call(other_kernel, in_specs=[pl.BlockSpec(memory_space=pltpu.HB...  3.36 us
    pallas_call x1, Pallas kernels, own(): pl.pallas_call(own_kernel, in_specs=[near] * 3, out_specs=near, out_shape...  1.95 us
    ppermute x1, starting transfers between devices, on_device(): came = lax.ppermute(other, 'c', [(0, 1), (1, 0)])  1.92 us
  transfers between devices with their start and end apart: 1, of which 1 were waited for; matrix products, arithmetic and copies ran while one was open for 0% of the time, Pallas kernels for 4%

profile of v4, /device:TPU:8, one launch (start us, length us, event | category | flops | bytes accessed | tf_op | source)
XLA Modules:
  0.0 58.1 jit_solution(4051769337408478965)
XLA Ops:
  0.0 0.0 copy-start
  0.0 3.4 %shard_map.64 = (bf16[128,4096]{1,0:T(8,128)(2,1)S(1)}, s32[1,64]{1,0:T(1,128)S(1)}, bf16[2,128,128]{2,1,0:T(8,128)(2,1)S(1)}, bf16[2,128,2,4096]{3,2,1,0:T(2,128)(2,1)S(1)}) custom-call(s32[1,64]{1,0:T(1,128)} %bitcast.8, bf16[2,128,128]{2,1,0:T(8,128)(2,1)} %table_hbm.1, bf16[2,128,2,4096]{3,2,1,0:T(2,128)(2,1)} %echo_hbm.1), custom_call_target="tpu_custom_call" | custom-call | tf_op jit(solution)/shard_map/pallas_call | solution.py:90
  3.4 1.9 %collective-permute-start = (bf16[128,4096]{1,0:T(8,128)(2,1)S(1)}, bf16[128,4096]{1,0:T(8,128)(2,1)S(1)}, u32[]{:S(2)}, u32[]{:S(2)}) collective-permute-start(bf16[128,4096]{1,0:T(8,128)(2,1)S(1)} %get-tuple-element.14), channel_id=1, source_target_pairs={{0,16},{16,0},{1,17},{17,1},{2,18},{18,2},{3,19},{19,3},{4,20},{20... | collective-permute-start | bytes 3145736 | tf_op jit(solution)/shard_map/ppermute | solution.py:232
  5.3 0.0 copy-done
  5.3 0.1 shard_map.66.band_ref
  5.4 2.0 %shard_map.65.own_ref = bf16[128,4096]{1,0:T(8,128)(2,1)S(1)} custom-call(s32[1,64]{1,0:T(1,128)S(1)} %get-tuple-element.11.index_ref, bf16[2,128,128]{2,1,0:T(8,128)(2,1)S(1)} %get-tuple-element.12.table_ref, bf16[2,128,2,4096]{3,2,1,0:T(2,128)(2,1)S(1)} %get-tuple-element.13.echo_ref), custom_call_target="tpu_custom_call" | custom-call | flops 1073741824 | bytes 4194304 | tf_op jit(solution)/shard_map/pallas_call | solution.py:100
  7.4 0.0 copy-start.1
  7.4 0.0 copy-start.2
  7.4 0.5 collective-permute-done.came_ref
  7.9 0.3 shard_map.67
  8.2 19.5 %all_to_all.10.parts_ref = bf16[4,32,4096]{2,1,0:T(8,128)(2,1)S(1)} all-to-all(bf16[4,32,4096]{2,1,0:T(8,128)(2,1)S(1)} %shard_map.67), channel_id=1, replica_groups=mesh['x'=4,'z'=4,'c'=2,'y'=8,'w'=2] {'x'}, dimensions={0} | all-to-all | bytes 2097152 | tf_op jit(solution)/shard_map/all_to_all | solution.py:236
  27.7 0.5 shard_map.68
  28.2 29.1 %all_to_all.11 = bf16[64,16,128]{2,1,0:T(8,128)(2,1)S(1)} all-to-all(bf16[64,16,128]{2,1,0:T(8,128)(2,1)S(1)} %bitcast.5), channel_id=1, replica_groups=mesh['x'=4,'z'=4,'c'=2,'y'=8,'w'=2] {'z','y','w'}, dimensions={0} | all-to-all | bytes 524288 | tf_op jit(solution)/shard_map/all_to_all | solution.py:238
  57.3 0.0 copy-done.1
  57.3 0.0 copy-done.2
  57.3 0.8 %shard_map.69 = f32[4,32,256]{2,1,0:T(8,128)} custom-call(f32[2,2]{1,0:T(2,128)S(1)} %copy-done.1, s32[1,2]{1,0:T(1,128)S(1)} %bitcast.7, bf16[4,16,16,128]{3,2,1,0:T(8,128)(2,1)S(1)} %bitcast.6), custom_call_target="tpu_custom_call" | custom-call | tf_op jit(solution)/shard_map/pallas_call | solution.py:219
Async XLA Ops:
  0.0 5.3 %copy-start = (bf16[2,256]{1,0:T(2,128)(2,1)S(1)}, bf16[2,256]{1,0:T(2,128)(2,1)}, u32[]{:S(2)}) copy-start(bf16[2,256]{1,0:T(2,128)(2,1)} %code_ref.1) | copy-start | bytes 3076
  3.4 4.6 %collective-permute-start = (bf16[128,4096]{1,0:T(8,128)(2,1)S(1)}, bf16[128,4096]{1,0:T(8,128)(2,1)S(1)}, u32[]{:S(2)}, u32[]{:S(2)}) collective-permute-start(bf16[128,4096]{1,0:T(8,128)(2,1)S(1)} %get-tuple-element.14), channel_id=1, source_target_pairs={{0,16},{16,0},{1,17},{17,1},{2,18},{18,2},{3,19},{19,3},{4,20},{20... | collective-permute-start | bytes 3145736 | tf_op jit(solution)/shard_map/ppermute | solution.py:232
  7.4 49.9 %copy-start.1 = (f32[2,2]{1,0:T(2,128)S(1)}, f32[2,2]{1,0:T(2,128)}, u32[]{:S(2)}) copy-start(f32[2,2]{1,0:T(2,128)} %taps_ref.1) | copy-start | bytes 52
  7.4 49.9 %copy-start.2 = (s32[2]{0:T(128)S(1)}, s32[2]{0:T(128)}, u32[]{:S(2)}) copy-start(s32[2]{0:T(128)} %param.11) | copy-start | bytes 28

commit v5 on v4

--- a/solution.py
+++ b/solution.py
@@ -51,25 +51,33 @@
 
 
 def other_kernel(index_hbm, table_hbm, echo_hbm, other_ref, index_ref, table_ref, echo_ref, done):
-    gates = echo_hbm.shape[3]
+    parts, elems, pulses, gates = echo_hbm.shape
     width = gates // ECHO_STEPS
+    pieces = [(step * width, part) for step in range(ECHO_STEPS) for part in range(parts)]
     small = [
-        pltpu.make_async_copy(index_hbm, index_ref, done.at[ECHO_STEPS]),
-        pltpu.make_async_copy(table_hbm, table_ref, done.at[ECHO_STEPS + 1]),
+        pltpu.make_async_copy(index_hbm, index_ref, done.at[len(pieces)]),
+        pltpu.make_async_copy(table_hbm, table_ref, done.at[len(pieces) + 1]),
     ]
-    spans = [slice(step * width, (step + 1) * width) for step in range(ECHO_STEPS)]
     large = [
-        pltpu.make_async_copy(echo_hbm.at[:, :, :, span], echo_ref.at[:, :, :, span], done.at[step])
-        for step, span in enumerate(spans)
+        pltpu.make_async_copy(
+            echo_hbm.at[part, :, :, first : first + width], echo_ref.at[part, :, :, first : first + width], done.at[i]
+        )
+        for i, (first, part) in enumerate(pieces)
     ]
     for copy in small + large:
         copy.start()
     for copy in small:
         copy.wait()
     weights = steering(table_ref, index_ref, other_ref.shape[0], 1 - lax.axis_index("c"))
-    for span, copy in zip(spans, large):
+    depth = elems * pulses
+    total = None
+    for (first, part), copy in zip(pieces, large):
         copy.wait()
-        other_ref[:, span] = beam_chunk(weights, echo_ref, span)
+        samples = echo_ref[part, :, :, first : first + width].reshape(depth, width)
+        term = jnp.dot(weights[:, part * depth : (part + 1) * depth], samples, preferred_element_type=f32)
+        total = term if part == 0 else total + term
+        if part == parts - 1:
+            other_ref[:, first : first + width] = total.astype(bf16)
 
 
 def own_kernel(index_ref, table_ref, echo_ref, own_ref):
@@ -92,7 +100,7 @@
         in_specs=[pl.BlockSpec(memory_space=pltpu.HBM)] * 3,
         out_specs=[near] * 4,
         out_shape=[partial] + [jax.ShapeDtypeStruct(a.shape, a.dtype) for a in operands],
-        scratch_shapes=[pltpu.SemaphoreType.DMA((ECHO_STEPS + 2,))],
+        scratch_shapes=[pltpu.SemaphoreType.DMA((2 * ECHO_STEPS + 2,))],
         compiler_params=pltpu.CompilerParams(vmem_limit_bytes=VMEM_BYTES),
     )(*(pltpu.with_memory_space_constraint(a, pltpu.HBM) for a in operands))
 

time: 58.3 us -> 58.1 us (level)
  no operation moved by 1% of the time
where the time goes in v5:
time: 58.1 us; the launch traced here: 57.9 us
  blocking collectives  48.5 us (83%)
  Pallas kernels  6.85 us (12%)
  starting transfers between devices  1.92 us (3%)
    all_to_all x1, blocking collectives, on_device(): blocks = lax.all_to_all(blocks, ('z', 'y', 'w'), 0, 0)  29.1 us
    all_to_all x1, blocking collectives, on_device(): parts = lax.all_to_all(added(own, came, x_count), 'x', 0, 0)  19.5 us
    pallas_call x1, Pallas kernels, beamform(): pl.pallas_call(other_kernel, in_specs=[pl.BlockSpec(memory_space=pltpu.HB...  3.13 us
    pallas_call x1, Pallas kernels, own(): pl.pallas_call(own_kernel, in_specs=[near] * 3, out_specs=near, out_shape...  1.95 us
    ppermute x1, starting transfers between devices, on_device(): came = lax.ppermute(other, 'c', [(0, 1), (1, 0)])  1.92 us
  transfers between devices with their start and end apart: 1, of which 1 were waited for; matrix products, arithmetic and copies ran while one was open for 0% of the time, Pallas kernels for 4%

profile of v5, /device:TPU:8, one launch (start us, length us, event | category | flops | bytes accessed | tf_op | source)
XLA Modules:
  0.0 57.9 jit_solution(11578189469932796878)
XLA Ops:
  0.0 0.0 copy-start
  0.0 3.1 %shard_map.64 = (bf16[128,4096]{1,0:T(8,128)(2,1)S(1)}, s32[1,64]{1,0:T(1,128)S(1)}, bf16[2,128,128]{2,1,0:T(8,128)(2,1)S(1)}, bf16[2,128,2,4096]{3,2,1,0:T(2,128)(2,1)S(1)}) custom-call(s32[1,64]{1,0:T(1,128)} %bitcast.8, bf16[2,128,128]{2,1,0:T(8,128)(2,1)} %table_hbm.1, bf16[2,128,2,4096]{3,2,1,0:T(2,128)(2,1)} %echo_hbm.1), custom_call_target="tpu_custom_call" | custom-call | tf_op jit(solution)/shard_map/pallas_call | solution.py:98
  3.1 1.9 %collective-permute-start = (bf16[128,4096]{1,0:T(8,128)(2,1)S(1)}, bf16[128,4096]{1,0:T(8,128)(2,1)S(1)}, u32[]{:S(2)}, u32[]{:S(2)}) collective-permute-start(bf16[128,4096]{1,0:T(8,128)(2,1)S(1)} %get-tuple-element.14), channel_id=1, source_target_pairs={{0,16},{16,0},{1,17},{17,1},{2,18},{18,2},{3,19},{19,3},{4,20},{20... | collective-permute-start | bytes 3145736 | tf_op jit(solution)/shard_map/ppermute | solution.py:240
  5.1 0.0 copy-done
  5.1 0.1 shard_map.66.band_ref
  5.2 1.9 %shard_map.65.own_ref = bf16[128,4096]{1,0:T(8,128)(2,1)S(1)} custom-call(s32[1,64]{1,0:T(1,128)S(1)} %get-tuple-element.11.index_ref, bf16[2,128,128]{2,1,0:T(8,128)(2,1)S(1)} %get-tuple-element.12.table_ref, bf16[2,128,2,4096]{3,2,1,0:T(2,128)(2,1)S(1)} %get-tuple-element.13.echo_ref), custom_call_target="tpu_custom_call" | custom-call | flops 1073741824 | bytes 4194304 | tf_op jit(solution)/shard_map/pallas_call | solution.py:108
  7.2 0.0 copy-start.1
  7.2 0.0 copy-start.2
  7.2 0.5 collective-permute-done.came_ref
  7.7 0.3 shard_map.67
  8.0 19.5 %all_to_all.10.parts_ref = bf16[4,32,4096]{2,1,0:T(8,128)(2,1)S(1)} all-to-all(bf16[4,32,4096]{2,1,0:T(8,128)(2,1)S(1)} %shard_map.67), channel_id=1, replica_groups=mesh['x'=4,'z'=4,'c'=2,'y'=8,'w'=2] {'x'}, dimensions={0} | all-to-all | bytes 2097152 | tf_op jit(solution)/shard_map/all_to_all | solution.py:244
  27.5 0.5 shard_map.68
  28.0 29.1 %all_to_all.11 = bf16[64,16,128]{2,1,0:T(8,128)(2,1)S(1)} all-to-all(bf16[64,16,128]{2,1,0:T(8,128)(2,1)S(1)} %bitcast.5), channel_id=1, replica_groups=mesh['x'=4,'z'=4,'c'=2,'y'=8,'w'=2] {'z','y','w'}, dimensions={0} | all-to-all | bytes 524288 | tf_op jit(solution)/shard_map/all_to_all | solution.py:246
  57.1 0.0 copy-done.1
  57.1 0.0 copy-done.2
  57.1 0.8 %shard_map.69 = f32[4,32,256]{2,1,0:T(8,128)} custom-call(f32[2,2]{1,0:T(2,128)S(1)} %copy-done.1, s32[1,2]{1,0:T(1,128)S(1)} %bitcast.7, bf16[4,16,16,128]{3,2,1,0:T(8,128)(2,1)S(1)} %bitcast.6), custom_call_target="tpu_custom_call" | custom-call | tf_op jit(solution)/shard_map/pallas_call | solution.py:227
Async XLA Ops:
  0.0 5.1 %copy-start = (bf16[2,256]{1,0:T(2,128)(2,1)S(1)}, bf16[2,256]{1,0:T(2,128)(2,1)}, u32[]{:S(2)}) copy-start(bf16[2,256]{1,0:T(2,128)(2,1)} %code_ref.1) | copy-start | bytes 3076
  3.1 4.6 %collective-permute-start = (bf16[128,4096]{1,0:T(8,128)(2,1)S(1)}, bf16[128,4096]{1,0:T(8,128)(2,1)S(1)}, u32[]{:S(2)}, u32[]{:S(2)}) collective-permute-start(bf16[128,4096]{1,0:T(8,128)(2,1)S(1)} %get-tuple-element.14), channel_id=1, source_target_pairs={{0,16},{16,0},{1,17},{17,1},{2,18},{18,2},{3,19},{19,3},{4,20},{20... | collective-permute-start | bytes 3145736 | tf_op jit(solution)/shard_map/ppermute | solution.py:240
  7.2 49.9 %copy-start.1 = (f32[2,2]{1,0:T(2,128)S(1)}, f32[2,2]{1,0:T(2,128)}, u32[]{:S(2)}) copy-start(f32[2,2]{1,0:T(2,128)} %taps_ref.1) | copy-start | bytes 52
  7.2 49.9 %copy-start.2 = (s32[2]{0:T(128)S(1)}, s32[2]{0:T(128)}, u32[]{:S(2)}) copy-start(s32[2]{0:T(128)} %param.11) | copy-start | bytes 28

commit v6 on v5

--- a/solution.py
+++ b/solution.py
@@ -159,16 +159,13 @@
     signal = parts_ref[0].astype(f32)
     for source in range(1, sources):
         signal += parts_ref[source].astype(f32)
-    imag = lax.rem(iota(signal.shape, 0), 2) == 1
-    turned = jnp.where(imag, -pltpu.roll(signal, 1, 0), pltpu.roll(signal, rows - 1, 0))
-    past = jnp.zeros((rows, taps), bf16)
-    total = None
-    for part, values in enumerate((signal, turned)):
-        values = jnp.concatenate([values.astype(bf16), past], 1)
-        windows = [values[:, slab * taps : (slab + 2) * taps] for slab in range(slabs)]
-        windows = jnp.concatenate(windows, 0)
-        product = lax.dot_general(windows, band_ref[part], LAST, preferred_element_type=f32)
-        total = product if total is None else total + product
+    values = jnp.concatenate([signal.astype(bf16), jnp.zeros((rows, taps), bf16)], 1)
+    windows = jnp.concatenate([values[:, slab * taps : (slab + 2) * taps] for slab in range(slabs)], 0)
+    by_real, by_imag = (
+        lax.dot_general(windows, band_ref[part], LAST, preferred_element_type=f32) for part in range(2)
+    )
+    imag = lax.rem(iota(by_imag.shape, 0), 2) == 1
+    total = by_real + jnp.where(imag, -pltpu.roll(by_imag, 1, 0), pltpu.roll(by_imag, rows * slabs - 1, 0))
     total = total.reshape(slabs, chips, PAIR, taps)
     for slab in range(slabs):
         block = total[slab]

time: 58.1 us -> 58 us (level)
  no operation moved by 1% of the time
where the time goes in v6:
time: 58 us; the launch traced here: 57.8 us
  blocking collectives  48.5 us (84%)
  Pallas kernels  6.8 us (12%)
  starting transfers between devices  1.92 us (3%)
    all_to_all x1, blocking collectives, on_device(): blocks = lax.all_to_all(blocks, ('z', 'y', 'w'), 0, 0)  29.1 us
    all_to_all x1, blocking collectives, on_device(): parts = lax.all_to_all(added(own, came, x_count), 'x', 0, 0)  19.5 us
    pallas_call x1, Pallas kernels, beamform(): pl.pallas_call(other_kernel, in_specs=[pl.BlockSpec(memory_space=pltpu.HB...  3.13 us
    pallas_call x1, Pallas kernels, own(): pl.pallas_call(own_kernel, in_specs=[near] * 3, out_specs=near, out_shape...  1.95 us
    ppermute x1, starting transfers between devices, on_device(): came = lax.ppermute(other, 'c', [(0, 1), (1, 0)])  1.92 us
  transfers between devices with their start and end apart: 1, of which 1 were waited for; matrix products, arithmetic and copies ran while one was open for 0% of the time, Pallas kernels for 4%

profile of v6, /device:TPU:8, one launch (start us, length us, event | category | flops | bytes accessed | tf_op | source)
XLA Modules:
  0.0 57.8 jit_solution(15010614772350844305)
XLA Ops:
  0.0 0.0 copy-start
  0.0 3.1 %shard_map.64 = (bf16[128,4096]{1,0:T(8,128)(2,1)S(1)}, s32[1,64]{1,0:T(1,128)S(1)}, bf16[2,128,128]{2,1,0:T(8,128)(2,1)S(1)}, bf16[2,128,2,4096]{3,2,1,0:T(2,128)(2,1)S(1)}) custom-call(s32[1,64]{1,0:T(1,128)} %bitcast.8, bf16[2,128,128]{2,1,0:T(8,128)(2,1)} %table_hbm.1, bf16[2,128,2,4096]{3,2,1,0:T(2,128)(2,1)} %echo_hbm.1), custom_call_target="tpu_custom_call" | custom-call | tf_op jit(solution)/shard_map/pallas_call | solution.py:98
  3.1 1.9 %collective-permute-start = (bf16[128,4096]{1,0:T(8,128)(2,1)S(1)}, bf16[128,4096]{1,0:T(8,128)(2,1)S(1)}, u32[]{:S(2)}, u32[]{:S(2)}) collective-permute-start(bf16[128,4096]{1,0:T(8,128)(2,1)S(1)} %get-tuple-element.14), channel_id=1, source_target_pairs={{0,16},{16,0},{1,17},{17,1},{2,18},{18,2},{3,19},{19,3},{4,20},{20... | collective-permute-start | bytes 3145736 | tf_op jit(solution)/shard_map/ppermute | solution.py:237
  5.1 0.0 copy-done
  5.1 0.1 shard_map.66.band_ref
  5.2 1.9 %shard_map.65.own_ref = bf16[128,4096]{1,0:T(8,128)(2,1)S(1)} custom-call(s32[1,64]{1,0:T(1,128)S(1)} %get-tuple-element.11.index_ref, bf16[2,128,128]{2,1,0:T(8,128)(2,1)S(1)} %get-tuple-element.12.table_ref, bf16[2,128,2,4096]{3,2,1,0:T(2,128)(2,1)S(1)} %get-tuple-element.13.echo_ref), custom_call_target="tpu_custom_call" | custom-call | flops 1073741824 | bytes 4194304 | tf_op jit(solution)/shard_map/pallas_call | solution.py:108
  7.2 0.0 copy-start.1
  7.2 0.0 copy-start.2
  7.2 0.5 collective-permute-done.came_ref
  7.7 0.3 shard_map.67
  8.0 19.5 %all_to_all.10.parts_ref = bf16[4,32,4096]{2,1,0:T(8,128)(2,1)S(1)} all-to-all(bf16[4,32,4096]{2,1,0:T(8,128)(2,1)S(1)} %shard_map.67), channel_id=1, replica_groups=mesh['x'=4,'z'=4,'c'=2,'y'=8,'w'=2] {'x'}, dimensions={0} | all-to-all | bytes 2097152 | tf_op jit(solution)/shard_map/all_to_all | solution.py:241
  27.5 0.5 shard_map.68
  28.0 29.1 %all_to_all.11 = bf16[64,16,128]{2,1,0:T(8,128)(2,1)S(1)} all-to-all(bf16[64,16,128]{2,1,0:T(8,128)(2,1)S(1)} %bitcast.5), channel_id=1, replica_groups=mesh['x'=4,'z'=4,'c'=2,'y'=8,'w'=2] {'z','y','w'}, dimensions={0} | all-to-all | bytes 524288 | tf_op jit(solution)/shard_map/all_to_all | solution.py:243
  57.0 0.0 copy-done.1
  57.0 0.0 copy-done.2
  57.0 0.8 %shard_map.69 = f32[4,32,256]{2,1,0:T(8,128)} custom-call(f32[2,2]{1,0:T(2,128)S(1)} %copy-done.1, s32[1,2]{1,0:T(1,128)S(1)} %bitcast.7, bf16[4,16,16,128]{3,2,1,0:T(8,128)(2,1)S(1)} %bitcast.6), custom_call_target="tpu_custom_call" | custom-call | tf_op jit(solution)/shard_map/pallas_call | solution.py:224
Async XLA Ops:
  0.0 5.1 %copy-start = (bf16[2,256]{1,0:T(2,128)(2,1)S(1)}, bf16[2,256]{1,0:T(2,128)(2,1)}, u32[]{:S(2)}) copy-start(bf16[2,256]{1,0:T(2,128)(2,1)} %code_ref.1) | copy-start | bytes 3076
  3.1 4.6 %collective-permute-start = (bf16[128,4096]{1,0:T(8,128)(2,1)S(1)}, bf16[128,4096]{1,0:T(8,128)(2,1)S(1)}, u32[]{:S(2)}, u32[]{:S(2)}) collective-permute-start(bf16[128,4096]{1,0:T(8,128)(2,1)S(1)} %get-tuple-element.14), channel_id=1, source_target_pairs={{0,16},{16,0},{1,17},{17,1},{2,18},{18,2},{3,19},{19,3},{4,20},{20... | collective-permute-start | bytes 3145736 | tf_op jit(solution)/shard_map/ppermute | solution.py:237
  7.2 49.8 %copy-start.1 = (f32[2,2]{1,0:T(2,128)S(1)}, f32[2,2]{1,0:T(2,128)}, u32[]{:S(2)}) copy-start(f32[2,2]{1,0:T(2,128)} %taps_ref.1) | copy-start | bytes 52
  7.2 49.8 %copy-start.2 = (s32[2]{0:T(128)S(1)}, s32[2]{0:T(128)}, u32[]{:S(2)}) copy-start(s32[2]{0:T(128)} %param.11) | copy-start | bytes 28

commit v7 on v6

--- a/solution.py
+++ b/solution.py
@@ -136,20 +136,9 @@
     )(pulse_code)
 
 
-def add_kernel(own_ref, came_ref, out_ref):
-    rows = out_ref.shape[1]
-    for chunk in range(out_ref.shape[0]):
-        here = slice(chunk * rows, (chunk + 1) * rows)
-        out_ref[chunk] = (own_ref[here].astype(f32) + came_ref[here].astype(f32)).astype(bf16)
-
-
 def added(own, came, chunks):
     rows, gates = own.shape
-    return pl.pallas_call(
-        add_kernel,
-        out_shape=jax.ShapeDtypeStruct((chunks, rows // chunks, gates), bf16),
-        compiler_params=pltpu.CompilerParams(vmem_limit_bytes=VMEM_BYTES),
-    )(own, came)
+    return (own.astype(f32) + came.astype(f32)).astype(bf16).reshape(chunks, rows // chunks, gates)
 
 
 def compress_kernel(parts_ref, band_ref, out_ref):

time: 58 us -> 58 us (level)
  no operation moved by 1% of the time
where the time goes in v7:
time: 58 us; the launch traced here: 57.9 us
  blocking collectives  48.5 us (84%)
  Pallas kernels  6.53 us (11%)
  starting transfers between devices  1.92 us (3%)
    all_to_all x1, blocking collectives, on_device(): blocks = lax.all_to_all(blocks, ('z', 'y', 'w'), 0, 0)  29.1 us
    all_to_all x1, blocking collectives, on_device(): parts = lax.all_to_all(added(own, came, x_count), 'x', 0, 0)  19.5 us
    pallas_call x1, Pallas kernels, beamform(): pl.pallas_call(other_kernel, in_specs=[pl.BlockSpec(memory_space=pltpu.HB...  3.13 us
    pallas_call x1, Pallas kernels, own(): pl.pallas_call(own_kernel, in_specs=[near] * 3, out_specs=near, out_shape...  1.95 us
    ppermute x1, starting transfers between devices, on_device(): came = lax.ppermute(other, 'c', [(0, 1), (1, 0)])  1.92 us
  transfers between devices with their start and end apart: 1, of which 1 were waited for; matrix products, arithmetic and copies ran while one was open for 0% of the time, Pallas kernels for 4%

profile of v7, /device:TPU:8, one launch (start us, length us, event | category | flops | bytes accessed | tf_op | source)
XLA Modules:
  0.0 57.9 jit_solution(17588042002618232447)
XLA Ops:
  0.0 0.0 copy-start
  0.0 3.1 %shard_map.64 = (bf16[128,4096]{1,0:T(8,128)(2,1)S(1)}, s32[1,64]{1,0:T(1,128)S(1)}, bf16[2,128,128]{2,1,0:T(8,128)(2,1)S(1)}, bf16[2,128,2,4096]{3,2,1,0:T(2,128)(2,1)S(1)}) custom-call(s32[1,64]{1,0:T(1,128)} %bitcast.10, bf16[2,128,128]{2,1,0:T(8,128)(2,1)} %table_hbm.1, bf16[2,128,2,4096]{3,2,1,0:T(2,128)(2,1)} %echo_hbm.1), custom_call_target="tpu_custom_call" | custom-call | tf_op jit(solution)/shard_map/pallas_call | solution.py:98
  3.1 1.9 %collective-permute-start = (bf16[128,4096]{1,0:T(8,128)(2,1)S(1)}, bf16[128,4096]{1,0:T(8,128)(2,1)S(1)}, u32[]{:S(2)}, u32[]{:S(2)}) collective-permute-start(bf16[128,4096]{1,0:T(8,128)(2,1)S(1)} %get-tuple-element.14), channel_id=1, source_target_pairs={{0,16},{16,0},{1,17},{17,1},{2,18},{18,2},{3,19},{19,3},{4,20},{20... | collective-permute-start | bytes 3145736 | tf_op jit(solution)/shard_map/ppermute | solution.py:226
  5.1 0.0 copy-done
  5.1 0.1 shard_map.66.band_ref
  5.2 1.9 %shard_map.65 = bf16[128,4096]{1,0:T(8,128)(2,1)S(1)} custom-call(s32[1,64]{1,0:T(1,128)S(1)} %get-tuple-element.11.index_ref, bf16[2,128,128]{2,1,0:T(8,128)(2,1)S(1)} %get-tuple-element.12.table_ref, bf16[2,128,2,4096]{3,2,1,0:T(2,128)(2,1)S(1)} %get-tuple-element.13.echo_ref), custom_call_target="tpu_custom_call" | custom-call | flops 1073741824 | bytes 4194304 | tf_op jit(solution)/shard_map/pallas_call | solution.py:108
  7.2 0.5 collective-permute-done
  7.7 0.2 add_convert_fusion
  7.9 0.0 copy-start.1
  8.0 0.0 copy-start.2
  8.0 19.5 %all_to_all.10.parts_ref = bf16[4,32,4096]{2,1,0:T(8,128)(2,1)S(1)} all-to-all(bf16[4,32,4096]{2,1,0:T(8,128)(2,1)S(1)} %bitcast.9), channel_id=1, replica_groups=mesh['x'=4,'z'=4,'c'=2,'y'=8,'w'=2] {'x'}, dimensions={0} | all-to-all | bytes 2097152 | tf_op jit(solution)/shard_map/all_to_all | solution.py:230
  27.5 0.5 shard_map.67
  28.0 29.1 %all_to_all.11 = bf16[64,16,128]{2,1,0:T(8,128)(2,1)S(1)} all-to-all(bf16[64,16,128]{2,1,0:T(8,128)(2,1)S(1)} %bitcast.6), channel_id=1, replica_groups=mesh['x'=4,'z'=4,'c'=2,'y'=8,'w'=2] {'z','y','w'}, dimensions={0} | all-to-all | bytes 524288 | tf_op jit(solution)/shard_map/all_to_all | solution.py:232
  57.0 0.0 copy-done.1
  57.0 0.0 copy-done.2
  57.0 0.8 %shard_map.68 = f32[4,32,256]{2,1,0:T(8,128)} custom-call(f32[2,2]{1,0:T(2,128)S(1)} %copy-done.1, s32[1,2]{1,0:T(1,128)S(1)} %bitcast.8, bf16[4,16,16,128]{3,2,1,0:T(8,128)(2,1)S(1)} %bitcast.7), custom_call_target="tpu_custom_call" | custom-call | tf_op jit(solution)/shard_map/pallas_call | solution.py:213
Async XLA Ops:
  0.0 5.1 %copy-start = (bf16[2,256]{1,0:T(2,128)(2,1)S(1)}, bf16[2,256]{1,0:T(2,128)(2,1)}, u32[]{:S(2)}) copy-start(bf16[2,256]{1,0:T(2,128)(2,1)} %code_ref.1) | copy-start | bytes 3076
  3.1 4.6 %collective-permute-start = (bf16[128,4096]{1,0:T(8,128)(2,1)S(1)}, bf16[128,4096]{1,0:T(8,128)(2,1)S(1)}, u32[]{:S(2)}, u32[]{:S(2)}) collective-permute-start(bf16[128,4096]{1,0:T(8,128)(2,1)S(1)} %get-tuple-element.14), channel_id=1, source_target_pairs={{0,16},{16,0},{1,17},{17,1},{2,18},{18,2},{3,19},{19,3},{4,20},{20... | collective-permute-start | bytes 3145736 | tf_op jit(solution)/shard_map/ppermute | solution.py:226
  7.9 49.1 %copy-start.1 = (f32[2,2]{1,0:T(2,128)S(1)}, f32[2,2]{1,0:T(2,128)}, u32[]{:S(2)}) copy-start(f32[2,2]{1,0:T(2,128)} %taps_ref.1) | copy-start | bytes 52
  8.0 49.1 %copy-start.2 = (s32[2]{0:T(128)S(1)}, s32[2]{0:T(128)}, u32[]{:S(2)}) copy-start(s32[2]{0:T(128)} %param.11) | copy-start | bytes 28

commit v8 on v7

--- a/solution.py
+++ b/solution.py
@@ -187,10 +187,11 @@
     return near, far
 
 
-def filter_kernel(taps_ref, dilation_ref, parts_ref, out_ref, value_ref):
+def filter_kernel(taps_ref, dilation_ref, parts_ref, out_ref, value_ref, side_ref, done):
     count, pairs = parts_ref.shape[:2]
     planes, pulses = out_ref.shape[:2]
     rows = pairs * PAIR
+    copies = []
     for side in range(2):
         here = slice(side * PAIR, (side + 1) * PAIR)
         total = parts_ref[0, :, here].astype(f32)
@@ -203,7 +204,12 @@
             value = value - taps_ref[section : section + 1, 0:1] * near - taps_ref[section : section + 1, 1:2] * far
         value_ref[...] = value
         for plane in range(planes):
-            out_ref[plane, :, side * LANES : (side + 1) * LANES] = value_ref[pl.ds(plane, pulses, stride=planes), :]
+            side_ref[side, plane] = value_ref[pl.ds(plane, pulses, stride=planes), :]
+        lanes = slice(side * LANES, (side + 1) * LANES)
+        copies.append(pltpu.make_async_copy(side_ref.at[side], out_ref.at[:, :, lanes], done.at[side]))
+        copies[side].start()
+    for copy in copies:
+        copy.wait()
 
 
 def clutter_filter(parts, clutter_taps, dilation):
@@ -213,8 +219,9 @@
     return pl.pallas_call(
         filter_kernel,
         in_specs=[near] * 3,
+        out_specs=pl.BlockSpec(memory_space=pltpu.HBM),
         out_shape=jax.ShapeDtypeStruct((planes, pulses, 2 * LANES), f32),
-        scratch_shapes=[pltpu.VMEM((pulses * planes, LANES), f32)],
+        scratch_shapes=[pltpu.VMEM((pulses * planes, LANES), f32), pltpu.VMEM((2, planes, pulses, LANES), f32), pltpu.SemaphoreType.DMA((2,))],
         compiler_params=pltpu.CompilerParams(vmem_limit_bytes=VMEM_BYTES),
     )(clutter_taps, dilation.reshape(1, -1), parts)
 

time: 58 us -> 58 us (level)
  no operation moved by 1% of the time
where the time goes in v8:
time: 58 us; the launch traced here: 57.9 us
  blocking collectives  48.5 us (84%)
  Pallas kernels  6.52 us (11%)
  starting transfers between devices  1.92 us (3%)
    all_to_all x1, blocking collectives, on_device(): blocks = lax.all_to_all(blocks, ('z', 'y', 'w'), 0, 0)  29.1 us
    all_to_all x1, blocking collectives, on_device(): parts = lax.all_to_all(added(own, came, x_count), 'x', 0, 0)  19.5 us
    pallas_call x1, Pallas kernels, beamform(): pl.pallas_call(other_kernel, in_specs=[pl.BlockSpec(memory_space=pltpu.HB...  3.13 us
    pallas_call x1, Pallas kernels, own(): pl.pallas_call(own_kernel, in_specs=[near] * 3, out_specs=near, out_shape...  1.95 us
    ppermute x1, starting transfers between devices, on_device(): came = lax.ppermute(other, 'c', [(0, 1), (1, 0)])  1.92 us
  transfers between devices with their start and end apart: 1, of which 1 were waited for; matrix products, arithmetic and copies ran while one was open for 0% of the time, Pallas kernels for 4%

profile of v8, /device:TPU:8, one launch (start us, length us, event | category | flops | bytes accessed | tf_op | source)
XLA Modules:
  0.0 57.9 jit_solution(2342151055759346853)
XLA Ops:
  0.0 0.0 copy-start
  0.0 3.1 %shard_map.64 = (bf16[128,4096]{1,0:T(8,128)(2,1)S(1)}, s32[1,64]{1,0:T(1,128)S(1)}, bf16[2,128,128]{2,1,0:T(8,128)(2,1)S(1)}, bf16[2,128,2,4096]{3,2,1,0:T(2,128)(2,1)S(1)}) custom-call(s32[1,64]{1,0:T(1,128)} %bitcast.10, bf16[2,128,128]{2,1,0:T(8,128)(2,1)} %table_hbm.1, bf16[2,128,2,4096]{3,2,1,0:T(2,128)(2,1)} %echo_hbm.1), custom_call_target="tpu_custom_call" | custom-call | tf_op jit(solution)/shard_map/pallas_call | solution.py:98
  3.1 1.9 %collective-permute-start = (bf16[128,4096]{1,0:T(8,128)(2,1)S(1)}, bf16[128,4096]{1,0:T(8,128)(2,1)S(1)}, u32[]{:S(2)}, u32[]{:S(2)}) collective-permute-start(bf16[128,4096]{1,0:T(8,128)(2,1)S(1)} %get-tuple-element.14), channel_id=1, source_target_pairs={{0,16},{16,0},{1,17},{17,1},{2,18},{18,2},{3,19},{19,3},{4,20},{20... | collective-permute-start | bytes 3145736 | tf_op jit(solution)/shard_map/ppermute | solution.py:233
  5.1 0.0 copy-done
  5.1 0.1 shard_map.66.band_ref
  5.2 1.9 %shard_map.65 = bf16[128,4096]{1,0:T(8,128)(2,1)S(1)} custom-call(s32[1,64]{1,0:T(1,128)S(1)} %get-tuple-element.11.index_ref, bf16[2,128,128]{2,1,0:T(8,128)(2,1)S(1)} %get-tuple-element.12.table_ref, bf16[2,128,2,4096]{3,2,1,0:T(2,128)(2,1)S(1)} %get-tuple-element.13.echo_ref), custom_call_target="tpu_custom_call" | custom-call | flops 1073741824 | bytes 4194304 | tf_op jit(solution)/shard_map/pallas_call | solution.py:108
  7.2 0.5 collective-permute-done
  7.7 0.2 add_convert_fusion
  7.9 0.0 copy-start.1
  8.0 0.0 copy-start.2
  8.0 19.5 %all_to_all.10.parts_ref = bf16[4,32,4096]{2,1,0:T(8,128)(2,1)S(1)} all-to-all(bf16[4,32,4096]{2,1,0:T(8,128)(2,1)S(1)} %bitcast.9), channel_id=1, replica_groups=mesh['x'=4,'z'=4,'c'=2,'y'=8,'w'=2] {'x'}, dimensions={0} | all-to-all | bytes 2097152 | tf_op jit(solution)/shard_map/all_to_all | solution.py:237
  27.5 0.5 shard_map.67
  28.0 29.1 %all_to_all.11 = bf16[64,16,128]{2,1,0:T(8,128)(2,1)S(1)} all-to-all(bf16[64,16,128]{2,1,0:T(8,128)(2,1)S(1)} %bitcast.6), channel_id=1, replica_groups=mesh['x'=4,'z'=4,'c'=2,'y'=8,'w'=2] {'z','y','w'}, dimensions={0} | all-to-all | bytes 524288 | tf_op jit(solution)/shard_map/all_to_all | solution.py:239
  57.0 0.0 copy-done.1
  57.0 0.0 copy-done.2
  57.0 0.8 %shard_map.68 = f32[4,32,256]{2,1,0:T(8,128)} custom-call(f32[2,2]{1,0:T(2,128)S(1)} %copy-done.1, s32[1,2]{1,0:T(1,128)S(1)} %bitcast.8, bf16[4,16,16,128]{3,2,1,0:T(8,128)(2,1)S(1)} %bitcast.7), custom_call_target="tpu_custom_call" | custom-call | tf_op jit(solution)/shard_map/pallas_call | solution.py:219
Async XLA Ops:
  0.0 5.1 %copy-start = (bf16[2,256]{1,0:T(2,128)(2,1)S(1)}, bf16[2,256]{1,0:T(2,128)(2,1)}, u32[]{:S(2)}) copy-start(bf16[2,256]{1,0:T(2,128)(2,1)} %code_ref.1) | copy-start | bytes 3076
  3.1 4.6 %collective-permute-start = (bf16[128,4096]{1,0:T(8,128)(2,1)S(1)}, bf16[128,4096]{1,0:T(8,128)(2,1)S(1)}, u32[]{:S(2)}, u32[]{:S(2)}) collective-permute-start(bf16[128,4096]{1,0:T(8,128)(2,1)S(1)} %get-tuple-element.14), channel_id=1, source_target_pairs={{0,16},{16,0},{1,17},{17,1},{2,18},{18,2},{3,19},{19,3},{4,20},{20... | collective-permute-start | bytes 3145736 | tf_op jit(solution)/shard_map/ppermute | solution.py:233
  7.9 49.1 %copy-start.1 = (f32[2,2]{1,0:T(2,128)S(1)}, f32[2,2]{1,0:T(2,128)}, u32[]{:S(2)}) copy-start(f32[2,2]{1,0:T(2,128)} %taps_ref.1) | copy-start | bytes 52
  8.0 49.1 %copy-start.2 = (s32[2]{0:T(128)S(1)}, s32[2]{0:T(128)}, u32[]{:S(2)}) copy-start(s32[2]{0:T(128)} %param.11) | copy-start | bytes 28
